TPU v7x, 256 devices: a whole 4x4x8 slice. The times are simulated.
256 devices in a mesh: seq: 8 (over x, core), head: 32 (over z, y).
Axes of the slice: x: 4, y: 4, z: 8, core: 2. Of those that a mesh axis runs over, the one named last changes fastest.
Arguments:
- x_rows: bfloat16 [40960, 12288], P('seq', 'head'), may hold values from -16 to 16
- z_rows: bfloat16 [40960, 12288], P('seq', 'head'), may hold values from -6 to 6
- b_rows: bfloat16 [40960, 128], P('seq', 'head'), may hold values from -6 to 6
- c_rows: bfloat16 [40960, 128], P('seq', 'head'), may hold values from -0.5 to 0.5
- step_raw: float32 [40960, 192], P('seq', 'head'), may hold values from -4 to 4
- conv_x: bfloat16 [4, 12288], P(None, 'head'), may hold values from -3 to 3
- conv_b: bfloat16 [4, 128], P(None, 'head'), may hold values from -3 to 3
- conv_c: bfloat16 [4, 128], P(None, 'head'), may hold values from -3 to 3
- decay_rate: float32 [192], P('head'), may hold values from 0 to 1, as said below
- norm_gain: float32 [12288], P('head'), may hold values from 0.5 to 1.5
Outputs:
- normed: bfloat16 [40960, 12288], P('seq', 'head')
Inputs may be any that keep to these rules, and one draw needn't show every extreme that they name: `decay_rate`: positive rates.
All inputs are finite; a program needn't handle non-finite values.
Results may differ from a plain program's by a relative error of at most 0.011.
Values may be sent and summed in bfloat16 or wider, within the bound.
A program may use at most 128 MiB of HBM per device.

v0:
```python
import jax
import jax.numpy as jnp
from jax import lax
from jax.sharding import PartitionSpec as P

GROUP = 256


def shifted(value, axis, steps):
    count = lax.axis_size(axis)
    first, last = (max(0, -steps), min(count, count - steps))
    return lax.ppermute(value, axis, [(source, source + steps) for source in range(first, last)])


def carried_in(value, axis, join, neutral):
    count, mine = (lax.axis_size(axis), lax.axis_index(axis))
    pieces = jax.tree.map(lambda part: lax.all_gather(part, axis), value)
    subtotal = jax.tree.map(
        lambda part, zero: jnp.full_like(part, 0) + jnp.asarray(zero, part.dtype), value, neutral
    )

    def hop(position, subtotal):
        longer = join(subtotal, jax.tree.map(lambda part: part[position], pieces))
        return jax.tree.map(lambda new, old: jnp.where(position < mine, new, old), longer, subtotal)

    return lax.fori_loop(0, count - 1, hop, subtotal)


def conv_valid(padded, weights, length):
    total = jnp.zeros((length, padded.shape[1]), jnp.float32)
    for k in range(weights.shape[0]):
        total = total + weights[k].astype(jnp.float32)[None, :] * padded[k : k + length].astype(
            jnp.float32
        )
    return jax.nn.silu(total).astype(jnp.bfloat16)


def block_parts(x_block, b_block, c_block, step_block, cum_block):
    scores = jnp.dot(c_block, b_block.T, preferred_element_type=jnp.float32)
    order = jnp.arange(x_block.shape[0])
    causal = order[:, None] >= order[None, :]
    gap = cum_block.T[:, :, None] - cum_block.T[:, None, :]
    gap = jnp.where(causal[None], gap, -jnp.inf)
    mixing = (scores[None] * jnp.exp(gap) * step_block.T[:, None, :]).astype(jnp.bfloat16)
    diag = jnp.einsum("hts,shp->thp", mixing, x_block, preferred_element_type=jnp.float32)
    tail = jnp.exp(cum_block[-1][None, :] - cum_block) * step_block
    weighted = (tail[:, :, None] * x_block.astype(jnp.float32)).astype(jnp.bfloat16)
    block_state = jnp.einsum("shp,sn->hpn", weighted, b_block, preferred_element_type=jnp.float32)
    return (diag, block_state)


def join_states(earlier, later):
    return (earlier[0] + later[0], jnp.exp(later[0])[:, None, None] * earlier[1] + later[1])


def body(x_rows, z_rows, b_rows, c_rows, step_raw, conv_x, conv_b, conv_c, decay_rate, norm_gain):
    length = x_rows.shape[0]
    width = conv_x.shape[0]
    local_heads = decay_rate.shape[0]
    x_width = x_rows.shape[1]
    head_size = x_width // local_heads
    state_cols = b_rows.shape[1]
    tails = jnp.concatenate(
        [x_rows[length - width + 1 :], b_rows[length - width + 1 :], c_rows[length - width + 1 :]],
        axis=1,
    )
    before = shifted(tails, "seq", 1)
    ext_x = jnp.concatenate([before[:, :x_width], x_rows], axis=0)
    ext_b = jnp.concatenate([before[:, x_width : x_width + state_cols], b_rows], axis=0)
    ext_c = jnp.concatenate([before[:, x_width + state_cols :], c_rows], axis=0)
    xs = conv_valid(ext_x, conv_x, length)
    whole_b, whole_c, taps_b, taps_c = (
        lax.all_gather(ext_b, "head", axis=1, tiled=True),
        lax.all_gather(ext_c, "head", axis=1, tiled=True),
        lax.all_gather(conv_b, "head", axis=1, tiled=True),
        lax.all_gather(conv_c, "head", axis=1, tiled=True),
    )
    bs = conv_valid(whole_b, taps_b, length)
    cs = conv_valid(whole_c, taps_c, length)
    state_size = bs.shape[1]
    step = jax.nn.softplus(step_raw)
    log_decay = -step * decay_rate[None, :]
    count = length // GROUP
    c_blocks = cs.reshape(count, GROUP, state_size)
    pieces = (
        xs.reshape(count, GROUP, local_heads, head_size),
        bs.reshape(count, GROUP, state_size),
        c_blocks,
        step.reshape(count, GROUP, local_heads),
        log_decay.reshape(count, GROUP, local_heads),
    )

    def advance(state, piece):
        x_block, b_block, c_block, step_block, decay_block = piece
        cum = jnp.cumsum(decay_block, axis=0)
        diag, block_state = block_parts(x_block, b_block, c_block, step_block, cum)
        new_state = jnp.exp(cum[-1])[:, None, None] * state + block_state
        return (new_state, (diag.reshape(GROUP, x_width), state, cum))

    start = jnp.zeros((local_heads, head_size, state_size), jnp.float32)
    last_state, (diags, local_states, cums) = lax.scan(advance, start, pieces)
    block_totals = cums[:, -1, :]
    device_decay = jnp.sum(block_totals, axis=0)
    _, carry_in = carried_in(
        (device_decay, last_state),
        "seq",
        join_states,
        (jnp.zeros_like(device_decay), jnp.zeros_like(last_state)),
    )
    preceding = jnp.cumsum(block_totals, axis=0) - block_totals
    full_states = local_states + jnp.exp(preceding)[:, :, None, None] * carry_in[None]
    carried = (
        jnp.einsum(
            "chpn,ctn->cthp",
            full_states,
            c_blocks.astype(jnp.float32),
            precision=lax.Precision.HIGHEST,
        )
        * jnp.exp(cums)[:, :, :, None]
    )
    y_rows = (diags + carried.reshape(count, GROUP, x_width)).reshape(length, x_width)
    gated = y_rows * jax.nn.silu(z_rows.astype(jnp.float32))
    total = lax.psum(jnp.sum(gated * gated, axis=1), "head")
    mean_sq = total[:, None] / (lax.axis_size("head") * x_width)
    return (gated * lax.rsqrt(mean_sq + 1e-05) * norm_gain[None, :]).astype(jnp.bfloat16)


def solution(mesh):
    placed = (
        P("seq", "head"),
        P("seq", "head"),
        P("seq", "head"),
        P("seq", "head"),
        P("seq", "head"),
        P(None, "head"),
        P(None, "head"),
        P(None, "head"),
        P("head"),
        P("head"),
    )
    return jax.shard_map(
        body, mesh=mesh, in_specs=placed, out_specs=P("seq", "head"), check_vma=False
    )
```

profile of v0, /device:TPU:32, one launch (start us, length us, event | category | flops | bytes accessed | tf_op | source)
XLA Modules:
  0.0 559.4 jit_solution(4812512615691280514)
XLA Ops:
  9.2 1.7 collective-permute-start
  14.3 45.3 %all-gather.4 = bf16[32,4,4]{2,1,0:T(4,128)(2,1)S(1)} all-gather(bf16[1,4,4]{2,1,0:T(4,128)(2,1)S(1)} %bitcast.171), channel_id=1, replica_groups=mesh['seq'=8,'head'=32] {'head'}, dimensions={0}, use_global_device_ids=true | all-gather | bytes 1056 | tf_op jit(solution)/shard_map/all_gather | solution.py:76
  60.5 40.6 %all-gather.2 = bf16[32,4,4]{2,1,0:T(4,128)(2,1)S(1)} all-gather(bf16[1,4,4]{2,1,0:T(4,128)(2,1)S(1)} %bitcast.172), channel_id=1, replica_groups=mesh['seq'=8,'head'=32] {'head'}, dimensions={0}, use_global_device_ids=true | all-gather | bytes 1056 | tf_op jit(solution)/shard_map/all_gather | solution.py:75
  104.8 11.5 %multiply_convert_fusion.4 = bf16[5120,384]{1,0:T(8,128)(2,1)} fusion(bf16[5120,384]{1,0:T(8,128)(2,1)} %param.14, bf16[3,384]{1,0:T(4,128)(2,1)S(1)} %copy.147, f32[384]{0:T(512)S(1)} %get-tuple-element.282, f32[384]{0:T(512)S(1)} %get-tuple-element.283, f32[384]{0:T(512)S(1)} %get-tuple-element.281, f32[384]{0:T(512)S(1)} %get-tuple-element.280), kind=kLoop, calls=%fused_computation.49 | loop fusion | flops 49152000 | bytes 7872768 | tf_op jit(solution)/shard_map/convert_element_type | solution.py:35
  116.3 6.3 %copy.148 = bf16[5120,384]{0,1:T(8,128)(2,1)} copy(bf16[5120,384]{1,0:T(8,128)(2,1)} %multiply_convert_fusion.4) | data formatting | bytes 7864320 | tf_op jit(solution)/shard_map/convert_element_type | solution.py:35
  122.6 7.6 %reshape.106 = bf16[20,256,6,64]{1,0,3,2:T(8,128)(2,1)} reshape(bf16[5120,384]{0,1:T(8,128)(2,1)} %copy.148) | data formatting | bytes 7864320 | tf_op jit(solution)/shard_map/reshape | solution.py:86
  130.2 5.2 copy.155
  135.3 2.5 reshape.135
  137.8 3.0 multiply_convert_fusion.5
  140.9 1.8 copy.154
  142.6 40.3 %all-gather.12.cloned.1.call-done = bf16[32,4,5123]{2,1,0:T(4,128)(2,1)} async-done(((bf16[1,4,5123]{2,1,0:T(4,128)(2,1)}), bf16[32,4,5123]{2,1,0:T(4,128)(2,1)}) %all-gather.12.cloned.1.call-update) | async-done | bytes 1311504 | tf_op jit(solution)/shard_map/all_gather | solution.py:73
  182.9 2.5 reshape.131
  185.4 3.0 multiply_convert_fusion.6
  188.4 2.5 copy.151
  190.9 155.9 %while.31 = (s32[]{:T(128)}, f32[6,64,128]{2,1,0:T(8,128)S(1)}, f32[20,256,384]{1,2,0:T(8,128)}, f32[20,6,64,128]{3,2,1,0:T(8,128)}, f32[20,256,6]{1,2,0:T(8,128...) while((s32[]{:T(128)}, f32[6,64,128]{2,1,0:T(8,128)S(1)}, ...), condition=%wide.region_3.4_spmd.clone, body=%wide.region_0.3_spmd.clone.sunk | while | flops 94997520 | bytes 3352916 | solution.py:101
  190.9 1.8 reduce-window.14
  198.7 1.8 reduce-window.14
  202.0 1.5 fusion.55
  206.5 1.8 reduce-window.14
  214.2 1.8 reduce-window.14
  222.1 1.8 reduce-window.14
  229.8 1.8 reduce-window.14
  237.7 1.8 reduce-window.14
  245.4 1.8 reduce-window.14
  253.2 1.8 reduce-window.14
  261.0 1.8 reduce-window.14
  264.3 1.5 fusion.55
  268.8 1.8 reduce-window.14
  276.6 1.8 reduce-window.14
  284.4 1.8 reduce-window.14
  287.7 1.5 fusion.55
  292.2 1.8 reduce-window.14
  300.0 1.8 reduce-window.14
  307.8 1.8 reduce-window.14
  315.6 1.8 reduce-window.14
  323.4 1.8 reduce-window.14
  331.2 1.8 reduce-window.14
  339.0 1.8 reduce-window.14
  342.3 1.5 fusion.55
  349.8 12.6 %all-reduce = f32[48]{0:T(128)S(1)} all-reduce(f32[48]{0:T(128)S(1)} %dynamic-update-slice), channel_id=2, replica_groups=mesh['seq'=8,'head'=32] {'seq'}, use_global_device_ids=true, to_apply=%add | all-reduce | flops 48 | bytes 384
  362.4 10.8 %all-gather.10.cloned.1.call-done = f32[48,64,128]{2,1,0:T(8,128)} async-done(((f32[6,64,128]{2,1,0:T(8,128)}), f32[48,64,128]{2,1,0:T(8,128)}) %all-gather.10.cloned.1.call-update) | async-done | bytes 1572880 | tf_op jit(solution)/shard_map/all_gather | solution.py:17
  373.2 7.4 %while.32 = (s32[]{:T(128)}, f32[6,64,128]{2,1,0:T(8,128)S(1)}, s32[]{:T(128)}, f32[8,6]{1,0:T(8,128)S(1)}, f32[8,6,64,128]{3,2,1,0:T(8,128)}, /*index=5*/s32[]{:T(128)}, s32[]{:T(128)}) while((s32[]{:T(128)}, f32[6,64,128]{2,1,0:T(8,128)S(1)}, s32[]{:T(128)}, f32[8,6]{1,0:T(8,128)S(1)}, f32[8,6,64,128]{3,2,1,0:T(8,128)}, ...), condition=%wide.region_7.8_spmd.clone, body=%wide.region_6.7_spmd.clone.sunk | while | flops 196612 | bytes 590001 | solution.py:26
  380.7 5.6 %broadcast_multiply_fusion = f32[20,256,6,64]{1,3,2,0:T(8,128)S(1)} fusion(f32[20,256,6]{1,2,0:T(8,128)S(1)} %exp.60, bf16[20,256,128,1]{2,1,3,0:T(8,128)(2,1)S(1)} %bitcast.159, f32[20,6,64,128]{3,2,1,0:T(8,128)} %get-tuple-element.155, f32[6,64,128]{2,1,0:T(8,128)S(1)} %get-tuple-element.158, f32[20,6]{1,0:T(8,128)S(1)} %subtract_exponential_fusion), kind=kOutput, calls=%fused_computation.55 | convolution fusion | flops 3023831040 | bytes 13427168 | tf_op jit(solution)/shard_map/chpn,ctn->cthp/dot_general | solution.py:113
  386.3 7.6 %bitcast_add_fusion.1 = f32[20,256,384]{1,2,0:T(8,128)} fusion(f32[20,256,384]{1,2,0:T(8,128)} %get-tuple-element.154, f32[20,256,6,64]{1,3,2,0:T(8,128)S(1)} %broadcast_multiply_fusion), kind=kLoop, calls=%fused_computation.46 | loop fusion | flops 1966080 | bytes 23592960 | tf_op jit(solution)/shard_map/add | solution.py:121
  393.9 9.1 %copy.159 = f32[20,256,384]{2,1,0:T(8,128)} copy(f32[20,256,384]{1,2,0:T(8,128)} %bitcast_add_fusion.1) | data formatting | bytes 15728640 | tf_op jit(solution)/shard_map/add | solution.py:121
  403.0 5.7 %multiply_reduce_fusion = f32[5120]{0:T(1024)S(1)} fusion(bf16[5120,384]{1,0:T(8,128)(2,1)} %param.15, f32[20,256,384]{2,1,0:T(8,128)} %copy.159), kind=kLoop, calls=%fused_computation.48 | loop fusion | flops 15723520 | bytes 11816960 | tf_op jit(solution)/shard_map/reduce_sum | solution.py:123
  408.7 137.0 %psum.7 = f32[5120]{0:T(1024)S(1)} all-reduce(f32[5120]{0:T(1024)S(1)} %multiply_reduce_fusion), channel_id=1, replica_groups=mesh['seq'=8,'head'=32] {'head'}, use_global_device_ids=true, to_apply=%region_9.10 | all-reduce | flops 5120 | bytes 40960 | tf_op jit(solution)/shard_map/psum | solution.py:123
  545.7 7.2 %multiply_convert_fusion.3 = bf16[5120,384]{1,0:T(8,128)(2,1)} fusion(f32[384]{0:T(512)S(1)} %copy-done.1, f32[5120]{0:T(1024)S(1)} %add_rsqrt_fusion, bf16[5120,384]{1,0:T(8,128)(2,1)} %param.15, f32[20,256,384]{2,1,0:T(8,128)} %copy.159), kind=kLoop, calls=%fused_computation.47 | loop fusion | flops 17694720 | bytes 15750656 | tf_op jit(solution)/shard_map/convert_element_type | solution.py:125
  (440 shorter events, 132.1 us)
Async XLA Ops:
  6.5 128.8 %all-gather.14.cloned.1.call-start = ((), (), s32[]{:S(2)}) async-start(), calls=%async_computation.2 | async-start | bytes 1385472 | tf_op jit(solution)/shard_map/all_gather | solution.py:74
  9.2 2.7 collective-permute-start
  13.4 169.5 %all-gather.12.cloned.1.call-start = ((), (), s32[]{:S(2)}) async-start(), calls=%async_computation.1 | async-start | bytes 1385472 | tf_op jit(solution)/shard_map/all_gather | solution.py:73
  104.7 268.5 %all-gather.10.cloned.1.call-start = ((), (), s32[]{:S(2)}) async-start(), calls=%async_computation | async-start | bytes 1769472 | tf_op jit(solution)/shard_map/all_gather | solution.py:17
  190.9 156.6 %copy-start.2 = (u32[256]{0:T(256)S(1)}, u32[256]{0:T(256)}, u32[]{:S(2)}) copy-start(u32[256]{0:T(256)} %constant.86) | copy-start | bytes 3076
  346.8 0.7 copy-start
  403.0 142.7 %copy-start.1 = (f32[384]{0:T(512)S(1)}, f32[384]{0:T(512)}, u32[]{:S(2)}) copy-start(f32[384]{0:T(512)} %param.23) | copy-start | bytes 4612
Sparse Core Ops, SparseCore 0:
  13.5 81.7 all-gather.13
  104.9 78.0 all-gather.11
  347.6 25.5 all-gather.9
where the time goes:
time: 568 us; the launch traced here: 559 us
  blocking collectives  236 us (42%)
  other arithmetic  105 us (18%)
  matrix products  79.7 us (14%)
  local copies, waits for them, and re-layouts  69.6 us (12%)
  waiting for transfers between devices  52 us (9%)
  between operations  13.9 us (2%)
    psum x1, blocking collectives, body(): total = lax.psum(jnp.sum(gated * gated, axis=1), 'head')  137 us
    all_gather x1, blocking collectives, body(): lax.all_gather(conv_c, 'head', axis=1, tiled=True)  45.3 us
    all_gather x1, blocking collectives, body(): lax.all_gather(conv_b, 'head', axis=1, tiled=True)  40.6 us
    all_gather x1, waiting for transfers between devices, body(): lax.all_gather(ext_b, 'head', axis=1, tiled=True)  40.3 us
    another operation x40, other arithmetic  37.3 us
    dot_general x20, matrix products, block_parts(): jnp.einsum('hts,shp->thp', mixing, x_block, preferred_element_type=jnp.fl...  30.6 us
    dot_general x20, matrix products, block_parts(): jnp.einsum('shp,sn->hpn', weighted, b_block, preferred_element_type=jnp.f...  23.1 us
    dot_general x20, matrix products, block_parts(): scores = jnp.dot(c_block, b_block.T, preferred_element_type=jnp.float32)  20.4 us
  transfers between devices with their start and end apart: 4, of which 3 were waited for; matrix products, arithmetic and copies ran while one was open for 8% of the time, Pallas kernels for 0%

commit v1 on v0

v1 whole, which is shorter than its diff:
```python
import functools

import jax
import jax.numpy as jnp
from jax import lax
from jax.experimental import pallas as pl
from jax.experimental.pallas import tpu as pltpu
from jax.sharding import PartitionSpec as P

GROUP = 256
HALF = 128
HEADS = 6
WIDTH = 384
LENGTH = 5120
BLOCKS = 20
CHUNKS = 4
PER = BLOCKS // CHUNKS
NSEQ = 8
NZ = 8
NY = 4
NHEAD = NZ * NY
STATE = 128
PART = STATE // NSEQ
HALO = 16
MASKED = -1e30
F32 = jnp.float32
BF16 = jnp.bfloat16


def remote(src, dst, send, recv, **where):
    return pltpu.make_async_remote_copy(
        src_ref=src,
        dst_ref=dst,
        send_sem=send,
        recv_sem=recv,
        device_id=where,
        device_id_type=pl.DeviceIdType.MESH,
    )


def loop(count, body):
    lax.fori_loop(0, count, lambda i, _: (body(i), 0)[1], 0)


def dot(a, b):
    return jnp.dot(a, b, preferred_element_type=F32)


def layer(
    x_hbm,
    z_hbm,
    b_ref,
    c_ref,
    raw_ref,
    taps_ref,
    small_ref,
    g_hbm,
    total_ref,
    xbuf,
    zbuf,
    xs_even,
    xs_odd,
    near,
    far,
    gath,
    cmat,
    score,
    ydiag,
    local_state,
    colq,
    rowq,
    bq,
    stepq,
    bcx,
    prec,
    state,
    payload,
    got,
    back,
    carry_in,
    ssrow,
    sspart,
    tot,
    x_sem,
    z_sem,
    g_sem,
    halo_send,
    halo_recv,
    zs_send,
    zs_recv,
    ys_send,
    ys_recv,
    yf_send,
    yf_recv,
    st_send,
    st_recv,
    cb_send,
    cb_recv,
    ss_send,
    ss_recv,
    tt_send,
    tt_recv,
):
    seq = lax.axis_index("seq")
    head = lax.axis_index("head")
    my_z = head // NY
    my_y = head % NY
    rows = LENGTH // CHUNKS

    def x_copy(c):
        part = pl.multiple_of(c * rows, rows)
        return pltpu.make_async_copy(
            x_hbm.at[pl.ds(part, rows)], xbuf.at[pl.ds(HALO + part, rows)], x_sem.at[c]
        )

    z_copy = pltpu.make_async_copy(z_hbm, zbuf, z_sem)

    barrier = pltpu.get_barrier_semaphore()

    def greet(r):
        pl.semaphore_signal(
            barrier,
            inc=1,
            device_id={"head": lax.rem(head + 1 + r, NHEAD)},
            device_id_type=pl.DeviceIdType.MESH,
        )

    def greet_seq(r):
        pl.semaphore_signal(
            barrier,
            inc=1,
            device_id={"seq": lax.rem(seq + 1 + r, NSEQ)},
            device_id_type=pl.DeviceIdType.MESH,
        )

    loop(NSEQ - 1, greet_seq)
    loop(NHEAD - 1, greet)
    for c in range(CHUNKS):
        x_copy(c).start()
    z_copy.start()

    bcx[0:4, HALF:] = b_ref[...].astype(F32)
    bcx[4:8, HALF:] = c_ref[...].astype(F32)
    raw = raw_ref[...]
    stepq[...] = jnp.ones_like(stepq)
    step_all = jnp.maximum(raw, 0.0) + jnp.log1p(jnp.exp(-jnp.abs(raw)))
    for i in range(BLOCKS):
        stepq[i, 0:HEADS, :] = step_all[:, GROUP * i : GROUP * (i + 1)]
    small = small_ref[...]

    pl.semaphore_wait(barrier, NHEAD - 1 + NSEQ - 1)

    def halo_bc():
        return remote(
            bcx.at[:, pl.ds(LENGTH, HALF)],
            bcx.at[:, pl.ds(0, HALF)],
            halo_send.at[0],
            halo_recv.at[0],
            seq=lax.rem(seq + 1, NSEQ),
        )

    def halo_x():
        return remote(
            x_hbm.at[pl.ds(LENGTH - HALO, HALO)],
            xbuf.at[pl.ds(0, HALO)],
            halo_send.at[1],
            halo_recv.at[1],
            seq=lax.rem(seq + 1, NSEQ),
        )

    @pl.when(seq < NSEQ - 1)
    def _():
        halo_bc().start()
        halo_x().start()

    step = stepq[...]
    rate = small[:, 4:5]
    decay = -(step * rate[None])
    decay = decay.reshape(BLOCKS * 8, GROUP)
    row = lax.broadcasted_iota(jnp.int32, (GROUP, GROUP), 0)
    col = lax.broadcasted_iota(jnp.int32, (GROUP, GROUP), 1)
    upper = jnp.where(row <= col, 1.0, 0.0).astype(BF16)
    high = decay.astype(BF16)
    rest = decay - high.astype(F32)
    mid = rest.astype(BF16)
    low = (rest - mid.astype(F32)).astype(BF16)
    cum = dot(high, upper) + (dot(mid, upper) + dot(low, upper))
    last = cum[:, GROUP - 1 : GROUP]
    step2 = step.reshape(BLOCKS * 8, GROUP)
    rowq[:, 0:8, :] = cum.reshape(BLOCKS, 8, GROUP)
    rowq[:, 8:16, :] = (jnp.exp(last - cum) * step2).reshape(BLOCKS, 8, GROUP)
    rowq[:, 16:24, :] = jnp.exp(cum).reshape(BLOCKS, 8, GROUP)
    bq[...] = (cum - jnp.log(step2)).reshape(BLOCKS, 8, GROUP)

    @pl.when(seq > 0)
    def _():
        halo_bc().wait_recv()
        halo_x().wait_recv()

    @pl.when(seq == 0)
    def _():
        bcx[:, 0:HALF] = jnp.zeros((8, HALF), F32)
        xbuf[0:HALO, :] = jnp.zeros((HALO, WIDTH), BF16)

    ext = bcx[...]
    acc = ext[:, HALF:] * small[:, 3:4]
    for back_by in (1, 2, 3):
        acc = acc + pltpu.roll(ext, back_by, axis=1)[:, HALF:] * small[:, 3 - back_by : 4 - back_by]
    acc = acc + acc * jnp.tanh(acc)
    for i in range(BLOCKS):
        tile = jnp.concatenate(
            [
                acc[:, GROUP * i : GROUP * i + HALF],
                acc[:, GROUP * i + HALF : GROUP * (i + 1)],
            ],
            axis=0,
        )
        place = HALF * (i % PER)
        gath[i // PER, my_y, my_z, :, place : place + HALF] = tile.astype(BF16)

    def z_send(c, r):
        return remote(
            gath.at[c, my_y, my_z],
            gath.at[c, my_y, my_z],
            zs_send.at[c, r],
            zs_recv.at[c, my_z],
            head=lax.rem(my_z + r, NZ) * NY + my_y,
        )

    def z_arrive(c, r):
        other = lax.rem(my_z + r, NZ)
        return remote(
            gath.at[c, my_y, other],
            gath.at[c, my_y, other],
            zs_send.at[c, r],
            zs_recv.at[c, other],
            head=other * NY + my_y,
        )

    order = (1, 7, 2, 6, 3, 5, 4)
    for c in range(CHUNKS):
        for r in order:
            z_send(c, r).start()

    above = lax.rem(my_y + 1, NY)
    below = lax.rem(my_y + NY - 1, NY)
    across = lax.rem(my_y + 2, NY)
    ups = my_z * NY + above
    downs = my_z * NY + below

    def y_up(c, slot):
        ref = gath.at[c, slot]
        return remote(ref, ref, ys_send.at[c, 0], ys_recv.at[c, 0], head=ups)

    def y_down(c, slot):
        ref = gath.at[c, slot]
        return remote(ref, ref, ys_send.at[c, 1], ys_recv.at[c, 1], head=downs)

    def f_up(c, slot):
        ref = gath.at[c, slot, pl.ds(0, NZ // 2)]
        return remote(ref, ref, yf_send.at[c, 0], yf_recv.at[c, 0], head=ups)

    def f_down(c, slot):
        ref = gath.at[c, slot, pl.ds(NZ // 2, NZ // 2)]
        return remote(ref, ref, yf_send.at[c, 1], yf_recv.at[c, 1], head=downs)

    def event_z(c):
        for r in order:
            z_arrive(c, r).wait_recv()
        y_up(c, my_y).start()
        y_down(c, my_y).start()

    def event_f(c):
        y_up(c, below).wait_recv()
        f_up(c, below).start()
        y_down(c, above).wait_recv()
        f_down(c, above).start()

    def event_d(c):
        f_up(c, across).wait_recv()
        f_down(c, across).wait_recv()

    taps = taps_ref[...].astype(F32) * 0.5
    lanes = lax.broadcasted_iota(jnp.int32, (GROUP, WIDTH), 1)
    even = (lanes & 127) < 64
    row1 = lax.broadcasted_iota(jnp.int32, (HALF, HALF), 0)
    col1 = lax.broadcasted_iota(jnp.int32, (HALF, HALF), 1)
    causal = row1 >= col1

    def phase1(i):
        base = pl.multiple_of(i * GROUP, GROUP)
        wide = xbuf[pl.ds(base, GROUP + HALO), :].astype(F32)
        half = wide[HALO:] * taps[3:4]
        for back_by in (1, 2, 3):
            half = half + pltpu.roll(wide, back_by, axis=0)[HALO:] * taps[3 - back_by : 4 - back_by]
        xs = half + half * jnp.tanh(half)
        xs_even[pl.ds(base, GROUP), :] = jnp.where(even, xs, 0.0).astype(BF16)
        xs_odd[pl.ds(base, GROUP), :] = jnp.where(even, 0.0, xs).astype(BF16)
        cols = rowq[i].T
        colq[i] = cols
        b_all = bq[i]
        for h in range(HEADS):
            a = cols[:, h : h + 1]
            b = b_all[h : h + 1, :]
            near[i, h] = jnp.exp(jnp.where(causal, a[:HALF] - b[:, :HALF], MASKED)).astype(BF16)
            far[i, h, :, 0:HALF] = jnp.exp(a[HALF:] - b[:, :HALF]).astype(BF16)
            far[i, h, :, HALF:] = jnp.exp(
                jnp.where(causal, a[HALF:] - b[:, HALF:], MASKED)
            ).astype(BF16)

    def step1(i):
        @pl.when(lax.rem(i, PER) == 0)
        def _():
            x_copy(i // PER).wait()

        phase1(i)

        @pl.when(i == 6)
        def _():
            event_z(0)

        @pl.when(i == 12)
        def _():
            event_z(1)
            event_f(0)

        @pl.when(i == 18)
        def _():
            event_z(2)
            event_f(1)

    loop(BLOCKS, step1)

    spread_row = lax.broadcasted_iota(jnp.int32, (24, WIDTH), 0)
    spread_col = lax.broadcasted_iota(jnp.int32, (24, WIDTH), 1) >> 6
    spread_w = jnp.where(spread_row == spread_col + 8, 1.0, 0.0).astype(BF16)
    spread_e = jnp.where(spread_row == spread_col + 16, 1.0, 0.0).astype(BF16)
    of_head = lax.broadcasted_iota(jnp.int32, (8, WIDTH), 1) >> 6
    upper4 = lax.broadcasted_iota(jnp.int32, (8, HALF), 0) < 4

    state[...] = jnp.zeros_like(state)
    prec[0] = jnp.ones((8, WIDTH), F32)

    def phase2(i):
        c = i // PER
        lane = pl.multiple_of(lax.rem(i, PER) * HALF, HALF)
        b_rows, c_rows = [], []
        for pair in range(NHEAD // 2):
            y, z = (2 * pair) // NZ, (2 * pair) % NZ
            first = gath[c, y, z, :, pl.ds(lane, HALF)].astype(F32)
            second = gath[c, y, z + 1, :, pl.ds(lane, HALF)].astype(F32)
            b_cols, c_cols = [], []
            for part in range(2):
                one = first[8 * part : 8 * part + 8]
                two = second[8 * part : 8 * part + 8]
                b_cols.append(jnp.where(upper4, one, pltpu.roll(two, 4, axis=0)))
                c_cols.append(jnp.where(upper4, pltpu.roll(one, 4, axis=0), two))
            b_rows.append(jnp.concatenate(b_cols, axis=1))
            c_rows.append(jnp.concatenate(c_cols, axis=1))
        b_t = jnp.concatenate(b_rows, axis=0).astype(BF16)
        c_i = jnp.concatenate(c_rows, axis=0).T.astype(BF16)
        cmat[i] = c_i
        score[i] = dot(c_i, b_t).astype(BF16)
        base = pl.multiple_of(i * GROUP, GROUP)
        xs = (xs_even[pl.ds(base, GROUP), :] + xs_odd[pl.ds(base, GROUP), :]).astype(F32)
        cols = colq[i]
        weight = dot(cols.astype(BF16), spread_w)
        new = dot(b_t, (weight * xs).astype(BF16))
        ends = cols[GROUP - 8 :, 16:24]
        gone = jnp.zeros((8, WIDTH), F32)
        for h in range(HEADS):
            gone = jnp.where(of_head == h, ends[7:8, h : h + 1], gone)
        old = state[...]
        local_state[i] = old
        state[...] = old * gone[0:1] + new
        prec[i + 1] = prec[i] * gone

    def phase3(i):
        base = pl.multiple_of(i * GROUP, GROUP)
        scores = score[i]
        top = scores[:HALF, :HALF]
        low_rows = scores[HALF:, :]
        for pair in range(HEADS // 2):
            span = slice(HALF * pair, HALF * (pair + 1))
            xe = xs_even[pl.ds(base, GROUP), span]
            xo = xs_odd[pl.ds(base, GROUP), span]
            m1 = jnp.concatenate([top * near[i, 2 * pair], top * near[i, 2 * pair + 1]], axis=1)
            x1 = jnp.concatenate([xe[:HALF], xo[:HALF]], axis=0)
            ydiag[pl.ds(base, HALF), span] = dot(m1, x1)
            m2 = jnp.concatenate(
                [low_rows * far[i, 2 * pair], low_rows * far[i, 2 * pair + 1]], axis=1
            )
            x2 = jnp.concatenate([xe, xo], axis=0)
            ydiag[pl.ds(base + HALF, HALF), span] = dot(m2, x2)

    def early(c):
        @pl.when(c == 0)
        def _():
            event_d(0)
            event_z(3)
            event_f(2)

        @pl.when(c == 1)
        def _():
            event_d(1)
            event_f(3)

        loop(PER, lambda j: phase2(c * PER + j))
        loop(PER, lambda j: phase3(c * PER + j))

    loop(2, early)

    def late(c):
        event_d(2 + c)
        loop(PER, lambda j: phase2((2 + c) * PER + j))

    loop(2, late)

    for j in range(NSEQ):
        payload[j, 0:PART, :] = state[PART * j : PART * (j + 1), :]
        payload[j, PART : PART + 8, :] = prec[BLOCKS]

    def st_copy(j, slot):
        return remote(payload.at[j], got.at[slot], st_send.at[j], st_recv.at[slot], seq=j)

    def cb_copy(j, slot):
        place = pl.multiple_of(slot * PART, PART)
        return remote(
            back.at[j], carry_in.at[pl.ds(place, PART)], cb_send.at[j], cb_recv.at[slot], seq=j
        )

    def others(count, me, body):
        loop(count - 1, lambda r: body(lax.rem(me + 1 + r, count)))

    others(NSEQ, seq, lambda j: st_copy(j, seq).start())
    got[seq] = payload[seq]
    loop(PER, lambda j: phase3(2 * PER + j))
    others(NSEQ, seq, lambda j: st_copy(j, j).wait_recv())
    carry = jnp.zeros((PART, WIDTH), F32)
    for j in range(NSEQ):
        back[j] = carry
        carry = carry * got[j, PART : PART + 1, :] + got[j, 0:PART, :]
    others(NSEQ, seq, lambda j: cb_copy(j, seq).start())
    carry_in[pl.ds(pl.multiple_of(seq * PART, PART), PART), :] = back[seq]
    loop(PER, lambda j: phase3(3 * PER + j))
    others(NSEQ, seq, lambda j: cb_copy(j, j).wait_recv())
    z_copy.wait()

    ones = jnp.ones((8, WIDTH), BF16)

    def g_copy(i):
        base = pl.multiple_of(i * GROUP, GROUP)
        return pltpu.make_async_copy(
            xbuf.at[pl.ds(HALO + base, GROUP)], g_hbm.at[pl.ds(base, GROUP)], g_sem.at[i]
        )

    def ss_copy(i):
        return remote(ssrow.at[i], sspart.at[head], ss_send.at[i], ss_recv.at[head], head=i)

    def ss_arrive(j):
        return remote(ssrow.at[0], sspart.at[j], ss_send.at[0], ss_recv.at[j], head=j)

    def tt_copy(j):
        return remote(tot.at[head], tot.at[head], tt_send.at[j], tt_recv.at[head], head=j)

    def tt_arrive(i):
        return remote(tot.at[i], tot.at[i], tt_send.at[0], tt_recv.at[i], head=i)

    def own_total():
        others(NHEAD, head, lambda j: ss_arrive(j).wait_recv())
        tot[head] = jnp.sum(sspart[...], axis=0)
        others(NHEAD, head, lambda j: tt_copy(j).start())

    def phase4(i):
        base = pl.multiple_of(i * GROUP, GROUP)
        whole = local_state[i] + carry_in[...] * prec[i][0:1]
        carried = dot(cmat[i], whole.astype(BF16))
        grown = dot(colq[i].astype(BF16), spread_e)
        y = ydiag[pl.ds(base, GROUP), :] + carried * grown
        half = zbuf[pl.ds(base, GROUP), :].astype(F32) * 0.5
        g = y * (half + half * jnp.tanh(half))
        xbuf[pl.ds(HALO + base, GROUP), :] = g.astype(BF16)
        g_copy(i).start()
        squares = (g * g).astype(BF16)
        sums = lax.dot_general(ones, squares, (((1,), (1,)), ((), ())), preferred_element_type=F32)
        ssrow[i] = sums[0:1]

        @pl.when(head == i)
        def _():
            sspart[head] = sums[0:1]

        @pl.when(head != i)
        def _():
            ss_copy(i).start()

        @pl.when(head == i - 2)
        def _():
            own_total()

    loop(BLOCKS, phase4)

    @pl.when((head == BLOCKS - 2) | (head == BLOCKS - 1))
    def _():
        own_total()

    @pl.when(seq < NSEQ - 1)
    def _():
        halo_bc().wait_send()
        halo_x().wait_send()

    def finish(c):
        for r in order:
            z_send(c, r).wait_send()
        y_up(c, my_y).wait_send()
        y_down(c, my_y).wait_send()
        f_up(c, below).wait_send()
        f_down(c, above).wait_send()

    loop(CHUNKS, finish)
    others(NSEQ, seq, lambda j: st_copy(j, seq).wait_send())
    others(NSEQ, seq, lambda j: cb_copy(j, seq).wait_send())

    def finish_block(i):
        g_copy(i).wait()

        @pl.when(head != i)
        def _():
            ss_copy(i).wait_send()
            tt_arrive(i).wait_recv()

    loop(BLOCKS, finish_block)

    @pl.when(head < BLOCKS)
    def _():
        others(NHEAD, head, lambda j: tt_copy(j).wait_send())

    total_ref[...] = tot[...]


def scale(g_ref, total_ref, gain_ref, out_ref):
    gain = gain_ref[...]
    for j in range(4):
        mean = total_ref[j] * (1.0 / (NHEAD * WIDTH))
        row = lax.rsqrt(mean + 1e-05)
        column = jnp.broadcast_to(row, (8, GROUP)).T[:, 0:1]
        rows = slice(GROUP * j, GROUP * (j + 1))
        out_ref[rows, :] = (g_ref[rows, :].astype(F32) * column * gain).astype(BF16)


def body(x_rows, z_rows, b_rows, c_rows, step_raw, conv_x, conv_b, conv_c, decay_rate, norm_gain):
    small = jnp.concatenate(
        [
            jnp.concatenate([conv_b, conv_c], axis=1).T.astype(F32) * 0.5,
            jnp.pad(decay_rate, (0, 2))[:, None],
            jnp.zeros((8, 3), F32),
        ],
        axis=1,
    )
    vmem = pl.BlockSpec(memory_space=pltpu.VMEM)
    hbm = pl.BlockSpec(memory_space=pl.ANY)
    dma = pltpu.SemaphoreType.DMA
    g, totals = pl.pallas_call(
        layer,
        out_shape=(
            jax.ShapeDtypeStruct((LENGTH, WIDTH), BF16),
            jax.ShapeDtypeStruct((BLOCKS, 1, GROUP), F32),
        ),
        in_specs=[hbm, hbm, vmem, vmem, vmem, vmem, vmem],
        out_specs=(hbm, vmem),
        scratch_shapes=[
            pltpu.VMEM((HALO + LENGTH, WIDTH), BF16),
            pltpu.VMEM((LENGTH, WIDTH), BF16),
            pltpu.VMEM((LENGTH, WIDTH), BF16),
            pltpu.VMEM((LENGTH, WIDTH), BF16),
            pltpu.VMEM((BLOCKS, HEADS, HALF, HALF), BF16),
            pltpu.VMEM((BLOCKS, HEADS, HALF, GROUP), BF16),
            pltpu.VMEM((CHUNKS, NY, NZ, 16, HALF * PER), BF16),
            pltpu.VMEM((BLOCKS, GROUP, STATE), BF16),
            pltpu.VMEM((BLOCKS, GROUP, GROUP), BF16),
            pltpu.VMEM((LENGTH, WIDTH), F32),
            pltpu.VMEM((BLOCKS, STATE, WIDTH), F32),
            pltpu.VMEM((BLOCKS, GROUP, 24), F32),
            pltpu.VMEM((BLOCKS, 24, GROUP), F32),
            pltpu.VMEM((BLOCKS, 8, GROUP), F32),
            pltpu.VMEM((BLOCKS, 8, GROUP), F32),
            pltpu.VMEM((8, HALF + LENGTH), F32),
            pltpu.VMEM((BLOCKS + 1, 8, WIDTH), F32),
            pltpu.VMEM((STATE, WIDTH), F32),
            pltpu.VMEM((NSEQ, PART + 8, WIDTH), F32),
            pltpu.VMEM((NSEQ, PART + 8, WIDTH), F32),
            pltpu.VMEM((NSEQ, PART, WIDTH), F32),
            pltpu.VMEM((STATE, WIDTH), F32),
            pltpu.VMEM((BLOCKS, 1, GROUP), F32),
            pltpu.VMEM((NHEAD, 1, GROUP), F32),
            pltpu.VMEM((BLOCKS, 1, GROUP), F32),
            dma((CHUNKS,)),
            dma,
            dma((BLOCKS,)),
            dma((2,)),
            dma((2,)),
            dma((CHUNKS, NZ)),
            dma((CHUNKS, NZ)),
            dma((CHUNKS, 2)),
            dma((CHUNKS, 2)),
            dma((CHUNKS, 2)),
            dma((CHUNKS, 2)),
            dma((NSEQ,)),
            dma((NSEQ,)),
            dma((NSEQ,)),
            dma((NSEQ,)),
            dma((BLOCKS,)),
            dma((NHEAD,)),
            dma((NHEAD,)),
            dma((BLOCKS,)),
        ],
        compiler_params=pltpu.CompilerParams(
            collective_id=0, has_side_effects=True, vmem_limit_bytes=60 * 2**20
        ),
        name="layer",
    )(x_rows, z_rows, b_rows.T, c_rows.T, step_raw.T, conv_x, small)
    return pl.pallas_call(
        scale,
        out_shape=jax.ShapeDtypeStruct((LENGTH, WIDTH), BF16),
        grid=(5,),
        in_specs=[
            pl.BlockSpec((1024, WIDTH), lambda i: (i, 0)),
            pl.BlockSpec((4, 1, GROUP), lambda i: (i, 0, 0)),
            pl.BlockSpec((1, WIDTH), lambda i: (0, 0)),
        ],
        out_specs=pl.BlockSpec((1024, WIDTH), lambda i: (i, 0)),
        name="scale",
    )(g, totals, norm_gain[None, :])


def solution(mesh):
    placed = (
        P("seq", "head"),
        P("seq", "head"),
        P("seq", "head"),
        P("seq", "head"),
        P("seq", "head"),
        P(None, "head"),
        P(None, "head"),
        P(None, "head"),
        P("head"),
        P("head"),
    )
    return jax.shard_map(
        body, mesh=mesh, in_specs=placed, out_specs=P("seq", "head"), check_vma=False
    )
```

time: 568 us -> 110 us (0.19); the launches traced: 559 us -> 109 us
  blocking collectives: 236 us -> 0 us
  Pallas kernels: 0 us -> 105 us
  other arithmetic: 105 us -> 0.68 us
  matrix products: 79.7 us -> 0 us
  local copies, waits for them, and re-layouts: 69.6 us -> 3.6 us
  waiting for transfers between devices: 52 us -> 0 us
  between operations: 13.9 us -> 0.01 us
    psum x1 -> x0, blocking collectives: 137 us -> none  [body(): total = lax.psum(jnp.sum(gated * gated, axis=1), 'head')]
    pallas_call x0 -> x2, Pallas kernels: none -> 105 us  [the longest x1 98.3 us: body(): pl.pallas_call(layer, out_shape=(jax.ShapeDtypeStruct((LENGTH, WIDTH), BF...]
    all_gather x2 -> x0, blocking collectives: 85.9 us -> none  [the longest x1 45.3 us: body(): lax.all_gather(conv_c, 'head', axis=1, tiled=True)]
    dot_general x61 -> x0, matrix products: 79.7 us -> none  [the longest x20 30.6 us: block_parts(): jnp.einsum('hts,shp->thp', mixing, x_block, preferred_element_type=jnp.fl...]
    all_gather x3 -> x0, waiting for transfers between devices: 51.1 us -> none  [the longest x1 40.3 us: body(): lax.all_gather(ext_b, 'head', axis=1, tiled=True)]
    another operation x42 -> x0, other arithmetic: 37.4 us -> none
    convert_element_type x4 -> x0, other arithmetic: 24.7 us -> none  [the longest x3 17.5 us: conv_valid(): return jax.nn.silu(total).astype(jnp.bfloat16)]
    dynamic_update_slice x40 -> x0, local copies, waits for them, and re-layouts: 15.8 us -> none  [body(): last_state, (diags, local_states, cums) = lax.scan(advance, start, pieces)]
  transfers between devices with their start and end apart: 4 -> 0, of which waited for: 3 -> 0; matrix products, arithmetic and copies ran while one was open for 8% -> 0% of each run, Pallas kernels for 0% -> 0%
where the time goes in v1:
time: 110 us; the launch traced here: 109 us
  Pallas kernels  105 us (95%)
  local copies, waits for them, and re-layouts  3.6 us (3%)
    pallas_call x1, Pallas kernels, body(): pl.pallas_call(layer, out_shape=(jax.ShapeDtypeStruct((LENGTH, WIDTH), BF...  98.3 us
    pallas_call x1, Pallas kernels, body(): pl.pallas_call(scale, out_shape=jax.ShapeDtypeStruct((LENGTH, WIDTH), BF1...  6.37 us

profile of v1, /device:TPU:32, one launch (start us, length us, event | category | flops | bytes accessed | tf_op | source)
XLA Modules:
  0.0 108.9 jit_solution(12069101175074396883)
XLA Ops:
  0.0 0.7 pad_bitcast_fusion
  0.7 0.1 pad.7.clone
  0.7 0.8 copy.11
  1.5 0.8 copy.12
  2.3 1.2 %broadcast_in_dim.7.gain_ref = f32[1,384]{1,0:T(1,128)} reshape(f32[384]{0:T(512)} %param.19) | data formatting | bytes 3072 | tf_op jit(solution)/shard_map/broadcast_in_dim | solution.py:632
  3.5 0.1 copy.13
  3.6 0.7 maximum_maximum_fusion.small_ref
  4.3 98.3 %layer.1 = (bf16[5120,384]{1,0:T(8,128)(2,1)}, f32[20,1,256]{2,1,0:T(1,128)}) custom-call(bf16[5120,384]{1,0:T(8,128)(2,1)} %x_hbm.1, bf16[5120,384]{1,0:T(8,128)(2,1)} %z_hbm.1, bf16[4,5120]{1,0:T(4,128)(2,1)} %bitcast.8, bf16[4,5120]{1,0:T(4,128)(2,1)} %bitcast.9, f32[6,5120]{1,0:T(8,128)} %bitcast.7, bf16[4,384]{1,0:T(4,128)(2,1)} %taps_ref.1, ...), custom_call_target="tpu_custom_call" | custom-call | tf_op jit(solution)/shard_map/layer/pallas_call | solution.py:562
  102.6 6.4 %scale.1 = bf16[5120,384]{1,0:T(8,128)(2,1)} custom-call(bf16[5120,384]{1,0:T(8,128)(2,1)} %get-tuple-element.7.g_ref, f32[20,1,256]{2,1,0:T(1,128)} %get-tuple-element.8.total_ref, f32[1,384]{1,0:T(1,128)} %broadcast_in_dim.7.gain_ref), custom_call_target="tpu_custom_call" | custom-call | tf_op jit(solution)/shard_map/scale/pallas_call | solution.py:621
  (2 shorter events, 0.0 us)

commit v2 on v1

--- a/solution.py
+++ b/solution.py
@@ -15,6 +15,8 @@
 BLOCKS = 20
 CHUNKS = 4
 PER = BLOCKS // CHUNKS
+SIDE = CHUNKS - 1
+SCALED = 4
 NSEQ = 8
 NZ = 8
 NY = 4
@@ -53,7 +55,9 @@
     c_ref,
     raw_ref,
     taps_ref,
-    small_ref,
+    taps_b_ref,
+    taps_c_ref,
+    rate_ref,
     g_hbm,
     total_ref,
     xbuf,
@@ -78,9 +82,10 @@
     got,
     back,
     carry_in,
-    ssrow,
-    sspart,
-    tot,
+    sums_row,
+    sums_z,
+    half_sums,
+    sums_y,
     x_sem,
     z_sem,
     g_sem,
@@ -96,10 +101,14 @@
     st_recv,
     cb_send,
     cb_recv,
-    ss_send,
-    ss_recv,
-    tt_send,
-    tt_recv,
+    side_out,
+    side_in,
+    ring_out,
+    ring_in,
+    sz_send,
+    sz_recv,
+    sy_send,
+    sy_recv,
 ):
     seq = lax.axis_index("seq")
     head = lax.axis_index("head")
@@ -117,24 +126,17 @@
 
     barrier = pltpu.get_barrier_semaphore()
 
-    def greet(r):
+    def greet(**where):
         pl.semaphore_signal(
-            barrier,
-            inc=1,
-            device_id={"head": lax.rem(head + 1 + r, NHEAD)},
-            device_id_type=pl.DeviceIdType.MESH,
-        )
-
-    def greet_seq(r):
-        pl.semaphore_signal(
-            barrier,
-            inc=1,
-            device_id={"seq": lax.rem(seq + 1 + r, NSEQ)},
-            device_id_type=pl.DeviceIdType.MESH,
-        )
-
-    loop(NSEQ - 1, greet_seq)
-    loop(NHEAD - 1, greet)
+            barrier, inc=1, device_id=where, device_id_type=pl.DeviceIdType.MESH
+        )
+
+    for r in range(1, NZ):
+        greet(head=lax.rem(my_z + r, NZ) * NY + my_y)
+    for r in range(1, NY):
+        greet(head=my_z * NY + lax.rem(my_y + r, NY))
+    for r in range(1, NSEQ):
+        greet(seq=lax.rem(seq + r, NSEQ))
     for c in range(CHUNKS):
         x_copy(c).start()
     z_copy.start()
@@ -146,9 +148,15 @@
     step_all = jnp.maximum(raw, 0.0) + jnp.log1p(jnp.exp(-jnp.abs(raw)))
     for i in range(BLOCKS):
         stepq[i, 0:HEADS, :] = step_all[:, GROUP * i : GROUP * (i + 1)]
-    small = small_ref[...]
-
-    pl.semaphore_wait(barrier, NHEAD - 1 + NSEQ - 1)
+    taps_bc = jnp.concatenate([taps_b_ref[...].astype(F32), taps_c_ref[...].astype(F32)], axis=1)
+    taps_bc = taps_bc.T * 0.5
+    head_row = lax.broadcasted_iota(jnp.int32, (8, GROUP), 0)
+    rate = jnp.zeros((8, GROUP), F32)
+    for h in range(HEADS):
+        rate = jnp.where(head_row == h, rate_ref[h], rate)
+    sums_row[...] = jnp.zeros_like(sums_row)
+
+    pl.semaphore_wait(barrier, NZ - 1 + NY - 1 + NSEQ - 1)
 
     def halo_bc():
         return remote(
@@ -174,7 +182,6 @@
         halo_x().start()
 
     step = stepq[...]
-    rate = small[:, 4:5]
     decay = -(step * rate[None])
     decay = decay.reshape(BLOCKS * 8, GROUP)
     row = lax.broadcasted_iota(jnp.int32, (GROUP, GROUP), 0)
@@ -203,9 +210,9 @@
         xbuf[0:HALO, :] = jnp.zeros((HALO, WIDTH), BF16)
 
     ext = bcx[...]
-    acc = ext[:, HALF:] * small[:, 3:4]
+    acc = ext[:, HALF:] * taps_bc[:, 3:4]
     for back_by in (1, 2, 3):
-        acc = acc + pltpu.roll(ext, back_by, axis=1)[:, HALF:] * small[:, 3 - back_by : 4 - back_by]
+        acc = acc + pltpu.roll(ext, back_by, axis=1)[:, HALF:] * taps_bc[:, 3 - back_by : 4 - back_by]
     acc = acc + acc * jnp.tanh(acc)
     for i in range(BLOCKS):
         tile = jnp.concatenate(
@@ -238,7 +245,19 @@
         )
 
     order = (1, 7, 2, 6, 3, 5, 4)
-    for c in range(CHUNKS):
+    def side_send(r):
+        ref = gath.at[SIDE, my_y, my_z]
+        there = my_z * NY + lax.rem(my_y + r, NY)
+        return remote(ref, ref, side_out.at[r], side_in.at[my_y], head=there)
+
+    def side_arrive(r):
+        other = lax.rem(my_y + r, NY)
+        ref = gath.at[SIDE, other, my_z]
+        return remote(ref, ref, side_out.at[r], side_in.at[other], head=my_z * NY + other)
+
+    for r in (1, 3, 2):
+        side_send(r).start()
+    for c in range(SIDE):
         for r in order:
             z_send(c, r).start()
 
@@ -263,6 +282,47 @@
     def f_down(c, slot):
         ref = gath.at[c, slot, pl.ds(NZ // 2, NZ // 2)]
         return remote(ref, ref, yf_send.at[c, 1], yf_recv.at[c, 1], head=downs)
+
+    z_above = lax.rem(my_z + 1, NZ) * NY + my_y
+    z_below = lax.rem(my_z + NZ - 1, NZ) * NY + my_y
+
+    def ring(hop, up, block):
+        half = NY // 2
+        if hop < NZ // 2 - 1:
+            ref = gath.at[SIDE, :, block]
+        elif up:
+            ref = gath.at[SIDE, pl.ds(0, half), block]
+        else:
+            ref = gath.at[SIDE, pl.ds(half, half), block]
+        way = 0 if up else 1
+        return remote(
+            ref,
+            ref,
+            ring_out.at[hop, way],
+            ring_in.at[hop, way],
+            head=z_above if up else z_below,
+        )
+
+    def ring_send(hop):
+        ring(hop, True, lax.rem(my_z + NZ - hop, NZ)).start()
+        ring(hop, False, lax.rem(my_z + hop, NZ)).start()
+
+    def ring_arrive(hop):
+        ring(hop, True, lax.rem(my_z + NZ - hop - 1, NZ)).wait_recv()
+        ring(hop, False, lax.rem(my_z + hop + 1, NZ)).wait_recv()
+
+    def ring_done(hop):
+        ring(hop, True, lax.rem(my_z + NZ - hop, NZ)).wait_send()
+        ring(hop, False, lax.rem(my_z + hop, NZ)).wait_send()
+
+    def event_side():
+        for r in (1, 3, 2):
+            side_arrive(r).wait_recv()
+        ring_send(0)
+
+    def event_ring(hop):
+        ring_arrive(hop - 1)
+        ring_send(hop)
 
     def event_z(c):
         for r in order:
@@ -315,19 +375,26 @@
 
         phase1(i)
 
-        @pl.when(i == 6)
+        @pl.when(i == 4)
+        def _():
+            event_side()
+
+        @pl.when(i == 9)
         def _():
             event_z(0)
 
         @pl.when(i == 12)
         def _():
+            event_ring(1)
+
+        @pl.when(i == 15)
+        def _():
             event_z(1)
+
+        @pl.when(i == 17)
+        def _():
             event_f(0)
-
-        @pl.when(i == 18)
-        def _():
-            event_z(2)
-            event_f(1)
+            event_ring(2)
 
     loop(BLOCKS, step1)
 
@@ -394,24 +461,32 @@
             ydiag[pl.ds(base + HALF, HALF), span] = dot(m2, x2)
 
     def early(c):
+        event_d(c)
+        loop(PER, lambda j: phase2(c * PER + j))
+
         @pl.when(c == 0)
         def _():
-            event_d(0)
-            event_z(3)
+            event_z(2)
+            event_f(1)
+            event_ring(3)
+
+        @pl.when(c == 1)
+        def _():
             event_f(2)
 
+        loop(PER, lambda j: phase3(c * PER + j))
+
+    loop(2, early)
+
+    def late(c):
+        @pl.when(c == 0)
+        def _():
+            event_d(2)
+
         @pl.when(c == 1)
         def _():
-            event_d(1)
-            event_f(3)
-
-        loop(PER, lambda j: phase2(c * PER + j))
-        loop(PER, lambda j: phase3(c * PER + j))
-
-    loop(2, early)
-
-    def late(c):
-        event_d(2 + c)
+            ring_arrive(NZ // 2 - 1)
+
         loop(PER, lambda j: phase2((2 + c) * PER + j))
 
     loop(2, late)
@@ -454,27 +529,82 @@
             xbuf.at[pl.ds(HALO + base, GROUP)], g_hbm.at[pl.ds(base, GROUP)], g_sem.at[i]
         )
 
-    def ss_copy(i):
-        return remote(ssrow.at[i], sspart.at[head], ss_send.at[i], ss_recv.at[head], head=i)
-
-    def ss_arrive(j):
-        return remote(ssrow.at[0], sspart.at[j], ss_send.at[0], ss_recv.at[j], head=j)
-
-    def tt_copy(j):
-        return remote(tot.at[head], tot.at[head], tt_send.at[j], tt_recv.at[head], head=j)
-
-    def tt_arrive(i):
-        return remote(tot.at[i], tot.at[i], tt_send.at[0], tt_recv.at[i], head=i)
-
-    def own_total():
-        others(NHEAD, head, lambda j: ss_arrive(j).wait_recv())
-        tot[head] = jnp.sum(sspart[...], axis=0)
-        others(NHEAD, head, lambda j: tt_copy(j).start())
+    parts = (pl.ds(0, 16), pl.ds(16, 8))
+
+    def sz_copy(p, r):
+        there = lax.rem(my_z + r, NZ) * NY + my_y
+        return remote(
+            sums_row.at[parts[p]],
+            sums_z.at[my_z, parts[p]],
+            sz_send.at[p, r],
+            sz_recv.at[p, my_z],
+            head=there,
+        )
+
+    def sz_arrive(p, r):
+        other = lax.rem(my_z + r, NZ)
+        return remote(
+            sums_row.at[parts[p]],
+            sums_z.at[other, parts[p]],
+            sz_send.at[p, r],
+            sz_recv.at[p, other],
+            head=other * NY + my_y,
+        )
+
+    def sy_copy(p, r):
+        there = my_z * NY + lax.rem(my_y + r, NY)
+        return remote(
+            half_sums.at[parts[p]],
+            sums_y.at[my_y, parts[p]],
+            sy_send.at[p, r],
+            sy_recv.at[p, my_y],
+            head=there,
+        )
+
+    def sy_arrive(p, r):
+        other = lax.rem(my_y + r, NY)
+        return remote(
+            half_sums.at[parts[p]],
+            sums_y.at[other, parts[p]],
+            sy_send.at[p, r],
+            sy_recv.at[p, other],
+            head=my_z * NY + other,
+        )
+
+    def sums_start(p):
+        for r in order:
+            sz_copy(p, r).start()
+        sums_z[my_z, parts[p], :] = sums_row[parts[p], :]
+
+    def sums_turn(p):
+        for r in order:
+            sz_arrive(p, r).wait_recv()
+        added = sums_z[0, parts[p], :]
+        for k in range(1, NZ):
+            added = added + sums_z[k, parts[p], :]
+        half_sums[parts[p], :] = added
+        sums_y[my_y, parts[p], :] = added
+        for r in (1, 3, 2):
+            sy_copy(p, r).start()
+
+    def sums_end(p):
+        for r in (1, 3, 2):
+            sy_arrive(p, r).wait_recv()
+        added = sums_y[0, parts[p], :]
+        for k in range(1, NY):
+            added = added + sums_y[k, parts[p], :]
+        total_ref[parts[p], :] = added
 
     def phase4(i):
         base = pl.multiple_of(i * GROUP, GROUP)
         whole = local_state[i] + carry_in[...] * prec[i][0:1]
-        carried = dot(cmat[i], whole.astype(BF16))
+        whole_high = whole.astype(BF16)
+        whole_low = (whole - whole_high.astype(F32)).astype(BF16)
+        c_i = cmat[i]
+        carried = dot(
+            jnp.concatenate([c_i, c_i], axis=1),
+            jnp.concatenate([whole_high, whole_low], axis=0),
+        )
         grown = dot(colq[i].astype(BF16), spread_e)
         y = ydiag[pl.ds(base, GROUP), :] + carried * grown
         half = zbuf[pl.ds(base, GROUP), :].astype(F32) * 0.5
@@ -483,25 +613,20 @@
         g_copy(i).start()
         squares = (g * g).astype(BF16)
         sums = lax.dot_general(ones, squares, (((1,), (1,)), ((), ())), preferred_element_type=F32)
-        ssrow[i] = sums[0:1]
-
-        @pl.when(head == i)
-        def _():
-            sspart[head] = sums[0:1]
-
-        @pl.when(head != i)
-        def _():
-            ss_copy(i).start()
-
-        @pl.when(head == i - 2)
-        def _():
-            own_total()
+        sums_row[pl.ds(jnp.where(i < 12, i, i + 4), 1), :] = sums[0:1]
+
+        @pl.when(i == 11)
+        def _():
+            sums_start(0)
+
+        @pl.when(i == 17)
+        def _():
+            sums_turn(0)
 
     loop(BLOCKS, phase4)
-
-    @pl.when((head == BLOCKS - 2) | (head == BLOCKS - 1))
-    def _():
-        own_total()
+    sums_start(1)
+    sums_end(0)
+    sums_turn(1)
 
     @pl.when(seq < NSEQ - 1)
     def _():
@@ -516,56 +641,63 @@
         f_up(c, below).wait_send()
         f_down(c, above).wait_send()
 
-    loop(CHUNKS, finish)
+    loop(SIDE, finish)
+    for r in (1, 3, 2):
+        side_send(r).wait_send()
+    for hop in range(NZ // 2):
+        ring_done(hop)
     others(NSEQ, seq, lambda j: st_copy(j, seq).wait_send())
     others(NSEQ, seq, lambda j: cb_copy(j, seq).wait_send())
 
-    def finish_block(i):
-        g_copy(i).wait()
-
-        @pl.when(head != i)
-        def _():
-            ss_copy(i).wait_send()
-            tt_arrive(i).wait_recv()
-
-    loop(BLOCKS, finish_block)
-
-    @pl.when(head < BLOCKS)
-    def _():
-        others(NHEAD, head, lambda j: tt_copy(j).wait_send())
-
-    total_ref[...] = tot[...]
-
-
-def scale(g_ref, total_ref, gain_ref, out_ref):
-    gain = gain_ref[...]
-    for j in range(4):
-        mean = total_ref[j] * (1.0 / (NHEAD * WIDTH))
-        row = lax.rsqrt(mean + 1e-05)
-        column = jnp.broadcast_to(row, (8, GROUP)).T[:, 0:1]
-        rows = slice(GROUP * j, GROUP * (j + 1))
-        out_ref[rows, :] = (g_ref[rows, :].astype(F32) * column * gain).astype(BF16)
+    loop(BLOCKS, lambda i: g_copy(i).wait())
+    for p in range(2):
+        for r in order:
+            sz_copy(p, r).wait_send()
+    sums_end(1)
+    for p in range(2):
+        for r in (1, 3, 2):
+            sy_copy(p, r).wait_send()
+
+
+def scale(g_hbm, total_ref, gain_ref, out_hbm, g_in, g_out, in_sem, out_sem):
+    rows = GROUP * SCALED
+
+    def come(k):
+        part = pl.ds(rows * k, rows)
+        return pltpu.make_async_copy(g_hbm.at[part], g_in.at[part], in_sem.at[k])
+
+    def go(k):
+        part = pl.ds(rows * k, rows)
+        return pltpu.make_async_copy(g_out.at[part], out_hbm.at[part], out_sem.at[k])
+
+    for k in range(BLOCKS // SCALED):
+        come(k).start()
+    gain = gain_ref[...][None, :]
+    factor = lax.rsqrt(total_ref[...] * (1.0 / (NHEAD * WIDTH)) + 1e-05).T
+    for k in range(BLOCKS // SCALED):
+        come(k).wait()
+        for j in range(SCALED * k, SCALED * (k + 1)):
+            place = j if j < 12 else j + 4
+            part = slice(GROUP * j, GROUP * (j + 1))
+            scaled = g_in[part, :].astype(F32) * factor[:, place : place + 1] * gain
+            g_out[part, :] = scaled.astype(BF16)
+        go(k).start()
+    for k in range(BLOCKS // SCALED):
+        go(k).wait()
 
 
 def body(x_rows, z_rows, b_rows, c_rows, step_raw, conv_x, conv_b, conv_c, decay_rate, norm_gain):
-    small = jnp.concatenate(
-        [
-            jnp.concatenate([conv_b, conv_c], axis=1).T.astype(F32) * 0.5,
-            jnp.pad(decay_rate, (0, 2))[:, None],
-            jnp.zeros((8, 3), F32),
-        ],
-        axis=1,
-    )
     vmem = pl.BlockSpec(memory_space=pltpu.VMEM)
     hbm = pl.BlockSpec(memory_space=pl.ANY)
+    smem = pl.BlockSpec(memory_space=pltpu.SMEM)
     dma = pltpu.SemaphoreType.DMA
     g, totals = pl.pallas_call(
         layer,
         out_shape=(
             jax.ShapeDtypeStruct((LENGTH, WIDTH), BF16),
-            jax.ShapeDtypeStruct((BLOCKS, 1, GROUP), F32),
+            jax.ShapeDtypeStruct((24, GROUP), F32),
         ),
-        in_specs=[hbm, hbm, vmem, vmem, vmem, vmem, vmem],
+        in_specs=[hbm, hbm, vmem, vmem, vmem, vmem, vmem, vmem, smem],
         out_specs=(hbm, vmem),
         scratch_shapes=[
             pltpu.VMEM((HALO + LENGTH, WIDTH), BF16),
@@ -590,9 +722,10 @@
             pltpu.VMEM((NSEQ, PART + 8, WIDTH), F32),
             pltpu.VMEM((NSEQ, PART, WIDTH), F32),
             pltpu.VMEM((STATE, WIDTH), F32),
-            pltpu.VMEM((BLOCKS, 1, GROUP), F32),
-            pltpu.VMEM((NHEAD, 1, GROUP), F32),
-            pltpu.VMEM((BLOCKS, 1, GROUP), F32),
+            pltpu.VMEM((24, GROUP), F32),
+            pltpu.VMEM((NZ, 24, GROUP), F32),
+            pltpu.VMEM((24, GROUP), F32),
+            pltpu.VMEM((NY, 24, GROUP), F32),
             dma((CHUNKS,)),
             dma,
             dma((BLOCKS,)),
@@ -608,28 +741,34 @@
             dma((NSEQ,)),
             dma((NSEQ,)),
             dma((NSEQ,)),
-            dma((BLOCKS,)),
-            dma((NHEAD,)),
-            dma((NHEAD,)),
-            dma((BLOCKS,)),
+            dma((NY,)),
+            dma((NY,)),
+            dma((NZ // 2, 2)),
+            dma((NZ // 2, 2)),
+            dma((2, NZ)),
+            dma((2, NZ)),
+            dma((2, NY)),
+            dma((2, NY)),
         ],
         compiler_params=pltpu.CompilerParams(
             collective_id=0, has_side_effects=True, vmem_limit_bytes=60 * 2**20
         ),
         name="layer",
-    )(x_rows, z_rows, b_rows.T, c_rows.T, step_raw.T, conv_x, small)
+    )(x_rows, z_rows, b_rows.T, c_rows.T, step_raw.T, conv_x, conv_b, conv_c, decay_rate)
     return pl.pallas_call(
         scale,
         out_shape=jax.ShapeDtypeStruct((LENGTH, WIDTH), BF16),
-        grid=(5,),
-        in_specs=[
-            pl.BlockSpec((1024, WIDTH), lambda i: (i, 0)),
-            pl.BlockSpec((4, 1, GROUP), lambda i: (i, 0, 0)),
-            pl.BlockSpec((1, WIDTH), lambda i: (0, 0)),
+        in_specs=[hbm, vmem, vmem],
+        out_specs=hbm,
+        scratch_shapes=[
+            pltpu.VMEM((LENGTH, WIDTH), BF16),
+            pltpu.VMEM((LENGTH, WIDTH), BF16),
+            dma((BLOCKS // SCALED,)),
+            dma((BLOCKS // SCALED,)),
         ],
-        out_specs=pl.BlockSpec((1024, WIDTH), lambda i: (i, 0)),
+        compiler_params=pltpu.CompilerParams(vmem_limit_bytes=60 * 2**20),
         name="scale",
-    )(g, totals, norm_gain[None, :])
+    )(g, totals, norm_gain)
 
 
 def solution(mesh):

time: 110 us -> 91.5 us (0.83)
  Pallas kernels: 105 us -> 91.2 us
  local copies, waits for them, and re-layouts: 3.6 us -> 0 us
    pallas_call x1, Pallas kernels: 98.3 us -> 87 us  [body(): pl.pallas_call(layer, out_shape=(jax.ShapeDtypeStruct((LENGTH, WIDTH), BF...]
    pallas_call x1, Pallas kernels: 6.37 us -> 4.13 us  [body(): pl.pallas_call(scale, out_shape=jax.ShapeDtypeStruct((LENGTH, WIDTH), BF1...]
    broadcast_in_dim x3 -> x0, local copies, waits for them, and re-layouts: 1.96 us -> none  [the longest x1 1.23 us: body(): norm_gain[None, :]]
    unnamed x2 -> x0, local copies, waits for them, and re-layouts: 1.56 us -> none
where the time goes in v2:
time: 91.5 us; the launch traced here: 91.2 us
  Pallas kernels  91.2 us (100%)
    pallas_call x1, Pallas kernels, body(): pl.pallas_call(layer, out_shape=(jax.ShapeDtypeStruct((LENGTH, WIDTH), BF...  87 us
    pallas_call x1, Pallas kernels, body(): pl.pallas_call(scale, out_shape=jax.ShapeDtypeStruct((LENGTH, WIDTH), BF1...  4.13 us

profile of v2, /device:TPU:32, one launch (start us, length us, event | category | flops | bytes accessed | tf_op | source)
XLA Modules:
  0.0 91.2 jit_solution(7972351941982840838)
XLA Ops:
  0.0 87.0 %layer.1 = (bf16[5120,384]{1,0:T(8,128)(2,1)}, f32[24,256]{1,0:T(8,128)}) custom-call(bf16[5120,384]{1,0:T(8,128)(2,1)} %x_hbm.1, bf16[5120,384]{1,0:T(8,128)(2,1)} %z_hbm.1, bf16[4,5120]{1,0:T(4,128)(2,1)} %bitcast.4, bf16[4,5120]{1,0:T(4,128)(2,1)} %bitcast.5, f32[6,5120]{1,0:T(8,128)} %bitcast.3, bf16[4,384]{1,0:T(4,128)(2,1)} %taps_ref.1, ...), custom_call_target="tpu_custom_call" | custom-call | tf_op jit(solution)/shard_map/layer/pallas_call | solution.py:694
  87.0 4.1 %scale.1 = bf16[5120,384]{1,0:T(8,128)(2,1)} custom-call(bf16[5120,384]{1,0:T(8,128)(2,1)} %get-tuple-element.7.g_hbm, f32[24,256]{1,0:T(8,128)} %get-tuple-element.8.total_ref, f32[384]{0:T(512)} %gain_ref.1), custom_call_target="tpu_custom_call" | custom-call | tf_op jit(solution)/shard_map/scale/pallas_call | solution.py:758

commit v3 on v2

--- a/solution.py
+++ b/solution.py
@@ -13,9 +13,11 @@
 WIDTH = 384
 LENGTH = 5120
 BLOCKS = 20
-CHUNKS = 4
-PER = BLOCKS // CHUNKS
-SIDE = CHUNKS - 1
+PAIRS = BLOCKS // 2
+LOADS = 4
+PER = BLOCKS // LOADS
+SPANS = ((0, 512), (512, 384))
+SIDE = (896, 384)
 SCALED = 4
 NSEQ = 8
 NZ = 8
@@ -68,7 +70,7 @@
     far,
     gath,
     cmat,
-    score,
+    bmat,
     ydiag,
     local_state,
     colq,
@@ -114,7 +116,7 @@
     head = lax.axis_index("head")
     my_z = head // NY
     my_y = head % NY
-    rows = LENGTH // CHUNKS
+    rows = LENGTH // LOADS
 
     def x_copy(c):
         part = pl.multiple_of(c * rows, rows)
@@ -137,7 +139,7 @@
         greet(head=my_z * NY + lax.rem(my_y + r, NY))
     for r in range(1, NSEQ):
         greet(seq=lax.rem(seq + r, NSEQ))
-    for c in range(CHUNKS):
+    for c in range(LOADS):
         x_copy(c).start()
     z_copy.start()
 
@@ -156,6 +158,22 @@
         rate = jnp.where(head_row == h, rate_ref[h], rate)
     sums_row[...] = jnp.zeros_like(sums_row)
 
+    def conv_bc(ext):
+        acc = ext * taps_bc[:, 3:4]
+        for back_by in (1, 2, 3):
+            acc = acc + pltpu.roll(ext, back_by, axis=1) * taps_bc[:, 3 - back_by : 4 - back_by]
+        return acc + acc * jnp.tanh(acc)
+
+    def put_tile(kind, pair, quarters):
+        tile = jnp.concatenate([q[4 * kind : 4 * kind + 4] for q in quarters], axis=0)
+        gath[kind, my_y, my_z, :, HALF * pair : HALF * (pair + 1)] = tile.astype(BF16)
+
+    acc = conv_bc(bcx[:, HALF:])
+    quarters = [acc[:, HALF * k : HALF * (k + 1)] for k in range(4 * PAIRS)]
+    for kind in range(2):
+        for pair in range(1, PAIRS):
+            put_tile(kind, pair, quarters[4 * pair : 4 * pair + 4])
+
     pl.semaphore_wait(barrier, NZ - 1 + NY - 1 + NSEQ - 1)
 
     def halo_bc():
@@ -180,6 +198,49 @@
     def _():
         halo_bc().start()
         halo_x().start()
+
+    def part(kind, y, z, span):
+        return gath.at[kind, y, z, :, pl.ds(*span)]
+
+    def z_send(kind, c, r):
+        ref = part(kind, my_y, my_z, SPANS[c])
+        there = lax.rem(my_z + r, NZ) * NY + my_y
+        return remote(ref, ref, zs_send.at[kind, c, r], zs_recv.at[kind, c, my_z], head=there)
+
+    def z_arrive(kind, c, r):
+        other = lax.rem(my_z + r, NZ)
+        ref = part(kind, my_y, other, SPANS[c])
+        return remote(
+            ref,
+            ref,
+            zs_send.at[kind, c, r],
+            zs_recv.at[kind, c, other],
+            head=other * NY + my_y,
+        )
+
+    order = (1, 7, 2, 6, 3, 5, 4)
+
+    def side_send(kind, r):
+        ref = part(kind, my_y, my_z, SIDE)
+        there = my_z * NY + lax.rem(my_y + r, NY)
+        return remote(ref, ref, side_out.at[kind, r], side_in.at[kind, my_y], head=there)
+
+    def side_arrive(kind, r):
+        other = lax.rem(my_y + r, NY)
+        ref = part(kind, other, my_z, SIDE)
+        return remote(
+            ref, ref, side_out.at[kind, r], side_in.at[kind, other], head=my_z * NY + other
+        )
+
+    y_order = (1, 3, 2)
+
+    def send_z(kind, c):
+        for r in order:
+            z_send(kind, c, r).start()
+
+    for r in y_order:
+        side_send(0, r).start()
+    send_z(0, 1)
 
     step = stepq[...]
     decay = -(step * rate[None])
@@ -199,146 +260,109 @@
     rowq[:, 16:24, :] = jnp.exp(cum).reshape(BLOCKS, 8, GROUP)
     bq[...] = (cum - jnp.log(step2)).reshape(BLOCKS, 8, GROUP)
 
-    @pl.when(seq > 0)
-    def _():
-        halo_bc().wait_recv()
-        halo_x().wait_recv()
-
-    @pl.when(seq == 0)
-    def _():
-        bcx[:, 0:HALF] = jnp.zeros((8, HALF), F32)
-        xbuf[0:HALO, :] = jnp.zeros((HALO, WIDTH), BF16)
-
-    ext = bcx[...]
-    acc = ext[:, HALF:] * taps_bc[:, 3:4]
-    for back_by in (1, 2, 3):
-        acc = acc + pltpu.roll(ext, back_by, axis=1)[:, HALF:] * taps_bc[:, 3 - back_by : 4 - back_by]
-    acc = acc + acc * jnp.tanh(acc)
-    for i in range(BLOCKS):
-        tile = jnp.concatenate(
-            [
-                acc[:, GROUP * i : GROUP * i + HALF],
-                acc[:, GROUP * i + HALF : GROUP * (i + 1)],
-            ],
-            axis=0,
-        )
-        place = HALF * (i % PER)
-        gath[i // PER, my_y, my_z, :, place : place + HALF] = tile.astype(BF16)
-
-    def z_send(c, r):
-        return remote(
-            gath.at[c, my_y, my_z],
-            gath.at[c, my_y, my_z],
-            zs_send.at[c, r],
-            zs_recv.at[c, my_z],
-            head=lax.rem(my_z + r, NZ) * NY + my_y,
-        )
-
-    def z_arrive(c, r):
-        other = lax.rem(my_z + r, NZ)
-        return remote(
-            gath.at[c, my_y, other],
-            gath.at[c, my_y, other],
-            zs_send.at[c, r],
-            zs_recv.at[c, other],
-            head=other * NY + my_y,
-        )
-
-    order = (1, 7, 2, 6, 3, 5, 4)
-    def side_send(r):
-        ref = gath.at[SIDE, my_y, my_z]
-        there = my_z * NY + lax.rem(my_y + r, NY)
-        return remote(ref, ref, side_out.at[r], side_in.at[my_y], head=there)
-
-    def side_arrive(r):
-        other = lax.rem(my_y + r, NY)
-        ref = gath.at[SIDE, other, my_z]
-        return remote(ref, ref, side_out.at[r], side_in.at[other], head=my_z * NY + other)
-
-    for r in (1, 3, 2):
-        side_send(r).start()
-    for c in range(SIDE):
-        for r in order:
-            z_send(c, r).start()
-
     above = lax.rem(my_y + 1, NY)
     below = lax.rem(my_y + NY - 1, NY)
     across = lax.rem(my_y + 2, NY)
     ups = my_z * NY + above
     downs = my_z * NY + below
 
-    def y_up(c, slot):
-        ref = gath.at[c, slot]
-        return remote(ref, ref, ys_send.at[c, 0], ys_recv.at[c, 0], head=ups)
-
-    def y_down(c, slot):
-        ref = gath.at[c, slot]
-        return remote(ref, ref, ys_send.at[c, 1], ys_recv.at[c, 1], head=downs)
-
-    def f_up(c, slot):
-        ref = gath.at[c, slot, pl.ds(0, NZ // 2)]
-        return remote(ref, ref, yf_send.at[c, 0], yf_recv.at[c, 0], head=ups)
-
-    def f_down(c, slot):
-        ref = gath.at[c, slot, pl.ds(NZ // 2, NZ // 2)]
-        return remote(ref, ref, yf_send.at[c, 1], yf_recv.at[c, 1], head=downs)
+    def y_copy(kind, c, slot, up):
+        ref = gath.at[kind, slot, :, :, pl.ds(*SPANS[c])]
+        way = 0 if up else 1
+        return remote(
+            ref,
+            ref,
+            ys_send.at[kind, c, way],
+            ys_recv.at[kind, c, way],
+            head=ups if up else downs,
+        )
+
+    def f_copy(kind, c, slot, up):
+        first = 0 if up else NZ // 2
+        ref = gath.at[kind, slot, pl.ds(first, NZ // 2), :, pl.ds(*SPANS[c])]
+        way = 0 if up else 1
+        return remote(
+            ref,
+            ref,
+            yf_send.at[kind, c, way],
+            yf_recv.at[kind, c, way],
+            head=ups if up else downs,
+        )
 
     z_above = lax.rem(my_z + 1, NZ) * NY + my_y
     z_below = lax.rem(my_z + NZ - 1, NZ) * NY + my_y
 
-    def ring(hop, up, block):
+    def ring(kind, hop, up, block):
         half = NY // 2
         if hop < NZ // 2 - 1:
-            ref = gath.at[SIDE, :, block]
+            ref = gath.at[kind, :, block, :, pl.ds(*SIDE)]
         elif up:
-            ref = gath.at[SIDE, pl.ds(0, half), block]
+            ref = gath.at[kind, pl.ds(0, half), block, :, pl.ds(*SIDE)]
         else:
-            ref = gath.at[SIDE, pl.ds(half, half), block]
+            ref = gath.at[kind, pl.ds(half, half), block, :, pl.ds(*SIDE)]
         way = 0 if up else 1
         return remote(
             ref,
             ref,
-            ring_out.at[hop, way],
-            ring_in.at[hop, way],
+            ring_out.at[kind, hop, way],
+            ring_in.at[kind, hop, way],
             head=z_above if up else z_below,
         )
 
-    def ring_send(hop):
-        ring(hop, True, lax.rem(my_z + NZ - hop, NZ)).start()
-        ring(hop, False, lax.rem(my_z + hop, NZ)).start()
-
-    def ring_arrive(hop):
-        ring(hop, True, lax.rem(my_z + NZ - hop - 1, NZ)).wait_recv()
-        ring(hop, False, lax.rem(my_z + hop + 1, NZ)).wait_recv()
-
-    def ring_done(hop):
-        ring(hop, True, lax.rem(my_z + NZ - hop, NZ)).wait_send()
-        ring(hop, False, lax.rem(my_z + hop, NZ)).wait_send()
-
-    def event_side():
-        for r in (1, 3, 2):
-            side_arrive(r).wait_recv()
-        ring_send(0)
-
-    def event_ring(hop):
-        ring_arrive(hop - 1)
-        ring_send(hop)
-
-    def event_z(c):
+    def ring_send(kind, hop):
+        ring(kind, hop, True, lax.rem(my_z + NZ - hop, NZ)).start()
+        ring(kind, hop, False, lax.rem(my_z + hop, NZ)).start()
+
+    def ring_arrive(kind, hop):
+        ring(kind, hop, True, lax.rem(my_z + NZ - hop - 1, NZ)).wait_recv()
+        ring(kind, hop, False, lax.rem(my_z + hop + 1, NZ)).wait_recv()
+
+    def ring_done(kind, hop):
+        ring(kind, hop, True, lax.rem(my_z + NZ - hop, NZ)).wait_send()
+        ring(kind, hop, False, lax.rem(my_z + hop, NZ)).wait_send()
+
+    def event_side(kind):
+        for r in y_order:
+            side_arrive(kind, r).wait_recv()
+        ring_send(kind, 0)
+
+    def event_ring(kind, hop):
+        ring_arrive(kind, hop - 1)
+        ring_send(kind, hop)
+
+    def event_z(kind, c):
         for r in order:
-            z_arrive(c, r).wait_recv()
-        y_up(c, my_y).start()
-        y_down(c, my_y).start()
-
-    def event_f(c):
-        y_up(c, below).wait_recv()
-        f_up(c, below).start()
-        y_down(c, above).wait_recv()
-        f_down(c, above).start()
-
-    def event_d(c):
-        f_up(c, across).wait_recv()
-        f_down(c, across).wait_recv()
+            z_arrive(kind, c, r).wait_recv()
+        y_copy(kind, c, my_y, True).start()
+        y_copy(kind, c, my_y, False).start()
+
+    def event_f(kind, c):
+        y_copy(kind, c, below, True).wait_recv()
+        f_copy(kind, c, below, True).start()
+        y_copy(kind, c, above, False).wait_recv()
+        f_copy(kind, c, above, False).start()
+
+    def event_d(kind, c):
+        f_copy(kind, c, across, True).wait_recv()
+        f_copy(kind, c, across, False).wait_recv()
+
+    def event_halo():
+        @pl.when(seq > 0)
+        def _():
+            halo_bc().wait_recv()
+            halo_x().wait_recv()
+
+        @pl.when(seq == 0)
+        def _():
+            bcx[:, 0:HALF] = jnp.zeros((8, HALF), F32)
+            xbuf[0:HALO, :] = jnp.zeros((HALO, WIDTH), BF16)
+
+        first = conv_bc(bcx[:, 0 : 2 * HALF])[:, HALF:]
+        for kind in range(2):
+            put_tile(kind, 0, [first] + quarters[1:4])
+        send_z(0, 0)
+        for r in y_order:
+            side_send(1, r).start()
 
     taps = taps_ref[...].astype(F32) * 0.5
     lanes = lax.broadcasted_iota(jnp.int32, (GROUP, WIDTH), 1)
@@ -350,12 +374,13 @@
     def phase1(i):
         base = pl.multiple_of(i * GROUP, GROUP)
         wide = xbuf[pl.ds(base, GROUP + HALO), :].astype(F32)
-        half = wide[HALO:] * taps[3:4]
-        for back_by in (1, 2, 3):
-            half = half + pltpu.roll(wide, back_by, axis=0)[HALO:] * taps[3 - back_by : 4 - back_by]
-        xs = half + half * jnp.tanh(half)
-        xs_even[pl.ds(base, GROUP), :] = jnp.where(even, xs, 0.0).astype(BF16)
-        xs_odd[pl.ds(base, GROUP), :] = jnp.where(even, 0.0, xs).astype(BF16)
+        once = pltpu.roll(wide, 1, axis=0)
+        older = pltpu.roll(wide * taps[1:2] + once * taps[0:1], 2, axis=0)
+        half = wide[HALO:] * taps[3:4] + once[HALO:] * taps[2:3] + older[HALO:]
+        xs = (half + half * jnp.tanh(half)).astype(BF16)
+        none = jnp.zeros_like(xs)
+        xs_even[pl.ds(base, GROUP), :] = jnp.where(even, xs, none)
+        xs_odd[pl.ds(base, GROUP), :] = jnp.where(even, none, xs)
         cols = rowq[i].T
         colq[i] = cols
         b_all = bq[i]
@@ -369,33 +394,31 @@
             ).astype(BF16)
 
     def step1(i):
-        @pl.when(lax.rem(i, PER) == 0)
+        block = lax.rem(i + 1, BLOCKS)
+
+        @pl.when((i == 0) | ((lax.rem(block, PER) == 0) & (block > 0)))
         def _():
-            x_copy(i // PER).wait()
-
-        phase1(i)
-
-        @pl.when(i == 4)
-        def _():
-            event_side()
-
-        @pl.when(i == 9)
-        def _():
-            event_z(0)
-
-        @pl.when(i == 12)
-        def _():
-            event_ring(1)
-
-        @pl.when(i == 15)
-        def _():
-            event_z(1)
-
-        @pl.when(i == 17)
-        def _():
-            event_f(0)
-            event_ring(2)
-
+            x_copy(block // PER).wait()
+
+        phase1(block)
+
+        for when, events in during.items():
+
+            @pl.when(i == when)
+            def _(events=events):
+                for event, *which in events:
+                    event(*which)
+
+    during = {
+        4: [(event_halo,)],
+        5: [(event_side, 0)],
+        7: [(event_z, 0, 1), (send_z, 1, 1)],
+        11: [(event_ring, 0, 1)],
+        12: [(event_z, 0, 0)],
+        14: [(event_f, 0, 1)],
+        16: [(event_ring, 0, 2), (send_z, 1, 0)],
+        17: [(event_side, 1)],
+    }
     loop(BLOCKS, step1)
 
     spread_row = lax.broadcasted_iota(jnp.int32, (24, WIDTH), 0)
@@ -408,88 +431,85 @@
     state[...] = jnp.zeros_like(state)
     prec[0] = jnp.ones((8, WIDTH), F32)
 
-    def phase2(i):
-        c = i // PER
-        lane = pl.multiple_of(lax.rem(i, PER) * HALF, HALF)
-        b_rows, c_rows = [], []
+    def assemble(kind, j):
+        lane = pl.multiple_of(j * HALF, HALF)
+        blocks = ([], [])
         for pair in range(NHEAD // 2):
             y, z = (2 * pair) // NZ, (2 * pair) % NZ
-            first = gath[c, y, z, :, pl.ds(lane, HALF)].astype(F32)
-            second = gath[c, y, z + 1, :, pl.ds(lane, HALF)].astype(F32)
-            b_cols, c_cols = [], []
-            for part in range(2):
-                one = first[8 * part : 8 * part + 8]
-                two = second[8 * part : 8 * part + 8]
-                b_cols.append(jnp.where(upper4, one, pltpu.roll(two, 4, axis=0)))
-                c_cols.append(jnp.where(upper4, pltpu.roll(one, 4, axis=0), two))
-            b_rows.append(jnp.concatenate(b_cols, axis=1))
-            c_rows.append(jnp.concatenate(c_cols, axis=1))
-        b_t = jnp.concatenate(b_rows, axis=0).astype(BF16)
-        c_i = jnp.concatenate(c_rows, axis=0).T.astype(BF16)
-        cmat[i] = c_i
-        score[i] = dot(c_i, b_t).astype(BF16)
+            first = gath[kind, y, z, :, pl.ds(lane, HALF)].astype(F32)
+            second = gath[kind, y, z + 1, :, pl.ds(lane, HALF)].astype(F32)
+            for e in range(2):
+                one = first[8 * e : 8 * e + 8]
+                two = second[8 * e : 8 * e + 8]
+                left = jnp.where(upper4, one, pltpu.roll(two, 4, axis=0))
+                right = jnp.where(upper4, pltpu.roll(one, 4, axis=0), two)
+                blocks[e].append(jnp.concatenate([left, right], axis=1))
+        return [jnp.concatenate(block, axis=0) for block in blocks]
+
+    def phase2(j):
+        for e, b_t in enumerate(assemble(0, j)):
+            i = 2 * j + e
+            b_t = b_t.astype(BF16)
+            bmat[i] = b_t
+            base = pl.multiple_of(i * GROUP, GROUP)
+            xs = (xs_even[pl.ds(base, GROUP), :] + xs_odd[pl.ds(base, GROUP), :]).astype(F32)
+            cols = colq[i]
+            weight = dot(cols.astype(BF16), spread_w)
+            new = dot(b_t, (weight * xs).astype(BF16))
+            ends = cols[GROUP - 8 :, 16:24]
+            gone = jnp.zeros((8, WIDTH), F32)
+            for h in range(HEADS):
+                gone = jnp.where(of_head == h, ends[7:8, h : h + 1], gone)
+            old = state[...]
+            local_state[i] = old
+            state[...] = old * gone[0:1] + new
+            prec[i + 1] = prec[i] * gone
+
+    def phase3(j):
+        for e, c_t in enumerate(assemble(1, j)):
+            i = 2 * j + e
+            c_i = c_t.T.astype(BF16)
+            cmat[i] = c_i
+            base = pl.multiple_of(i * GROUP, GROUP)
+            scores = dot(c_i, bmat[i]).astype(BF16)
+            top = scores[:HALF, :HALF]
+            low_rows = scores[HALF:, :]
+            for pair in range(HEADS // 2):
+                span = slice(HALF * pair, HALF * (pair + 1))
+                xe = xs_even[pl.ds(base, GROUP), span]
+                xo = xs_odd[pl.ds(base, GROUP), span]
+                m1 = jnp.concatenate(
+                    [top * near[i, 2 * pair], top * near[i, 2 * pair + 1]], axis=1
+                )
+                x1 = jnp.concatenate([xe[:HALF], xo[:HALF]], axis=0)
+                ydiag[pl.ds(base, HALF), span] = dot(m1, x1)
+                m2 = jnp.concatenate(
+                    [low_rows * far[i, 2 * pair], low_rows * far[i, 2 * pair + 1]], axis=1
+                )
+                x2 = jnp.concatenate([xe, xo], axis=0)
+                ydiag[pl.ds(base + HALF, HALF), span] = dot(m2, x2)
+
+    def gates(i):
         base = pl.multiple_of(i * GROUP, GROUP)
-        xs = (xs_even[pl.ds(base, GROUP), :] + xs_odd[pl.ds(base, GROUP), :]).astype(F32)
-        cols = colq[i]
-        weight = dot(cols.astype(BF16), spread_w)
-        new = dot(b_t, (weight * xs).astype(BF16))
-        ends = cols[GROUP - 8 :, 16:24]
-        gone = jnp.zeros((8, WIDTH), F32)
-        for h in range(HEADS):
-            gone = jnp.where(of_head == h, ends[7:8, h : h + 1], gone)
-        old = state[...]
-        local_state[i] = old
-        state[...] = old * gone[0:1] + new
-        prec[i + 1] = prec[i] * gone
-
-    def phase3(i):
-        base = pl.multiple_of(i * GROUP, GROUP)
-        scores = score[i]
-        top = scores[:HALF, :HALF]
-        low_rows = scores[HALF:, :]
-        for pair in range(HEADS // 2):
-            span = slice(HALF * pair, HALF * (pair + 1))
-            xe = xs_even[pl.ds(base, GROUP), span]
-            xo = xs_odd[pl.ds(base, GROUP), span]
-            m1 = jnp.concatenate([top * near[i, 2 * pair], top * near[i, 2 * pair + 1]], axis=1)
-            x1 = jnp.concatenate([xe[:HALF], xo[:HALF]], axis=0)
-            ydiag[pl.ds(base, HALF), span] = dot(m1, x1)
-            m2 = jnp.concatenate(
-                [low_rows * far[i, 2 * pair], low_rows * far[i, 2 * pair + 1]], axis=1
-            )
-            x2 = jnp.concatenate([xe, xo], axis=0)
-            ydiag[pl.ds(base + HALF, HALF), span] = dot(m2, x2)
-
-    def early(c):
-        event_d(c)
-        loop(PER, lambda j: phase2(c * PER + j))
-
-        @pl.when(c == 0)
-        def _():
-            event_z(2)
-            event_f(1)
-            event_ring(3)
-
-        @pl.when(c == 1)
-        def _():
-            event_f(2)
-
-        loop(PER, lambda j: phase3(c * PER + j))
-
-    loop(2, early)
-
-    def late(c):
-        @pl.when(c == 0)
-        def _():
-            event_d(2)
-
-        @pl.when(c == 1)
-        def _():
-            ring_arrive(NZ // 2 - 1)
-
-        loop(PER, lambda j: phase2((2 + c) * PER + j))
-
-    loop(2, late)
+        half = zbuf[pl.ds(base, GROUP), :].astype(F32) * 0.5
+        zbuf[pl.ds(base, GROUP), :] = (half + half * jnp.tanh(half)).astype(BF16)
+
+    event_f(0, 0)
+    event_z(1, 1)
+    z_copy.wait()
+    loop(BLOCKS // 2, gates)
+    event_ring(0, 3)
+    loop(BLOCKS // 2, lambda i: gates(BLOCKS // 2 + i))
+    event_ring(1, 1)
+    event_d(0, 0)
+    loop(4, phase2)
+    event_z(1, 0)
+    event_d(0, 1)
+    loop(3, lambda j: phase2(4 + j))
+    event_f(1, 1)
+    event_ring(1, 2)
+    ring_arrive(0, 3)
+    loop(3, lambda j: phase2(7 + j))
 
     for j in range(NSEQ):
         payload[j, 0:PART, :] = state[PART * j : PART * (j + 1), :]
@@ -509,7 +529,10 @@
 
     others(NSEQ, seq, lambda j: st_copy(j, seq).start())
     got[seq] = payload[seq]
-    loop(PER, lambda j: phase3(2 * PER + j))
+    event_f(1, 0)
+    event_ring(1, 3)
+    event_d(1, 1)
+    loop(3, lambda j: phase3(4 + j))
     others(NSEQ, seq, lambda j: st_copy(j, j).wait_recv())
     carry = jnp.zeros((PART, WIDTH), F32)
     for j in range(NSEQ):
@@ -517,9 +540,11 @@
         carry = carry * got[j, PART : PART + 1, :] + got[j, 0:PART, :]
     others(NSEQ, seq, lambda j: cb_copy(j, seq).start())
     carry_in[pl.ds(pl.multiple_of(seq * PART, PART), PART), :] = back[seq]
-    loop(PER, lambda j: phase3(3 * PER + j))
+    event_d(1, 0)
+    loop(4, phase3)
+    ring_arrive(1, 3)
+    loop(3, lambda j: phase3(7 + j))
     others(NSEQ, seq, lambda j: cb_copy(j, j).wait_recv())
-    z_copy.wait()
 
     ones = jnp.ones((8, WIDTH), BF16)
 
@@ -607,8 +632,7 @@
         )
         grown = dot(colq[i].astype(BF16), spread_e)
         y = ydiag[pl.ds(base, GROUP), :] + carried * grown
-        half = zbuf[pl.ds(base, GROUP), :].astype(F32) * 0.5
-        g = y * (half + half * jnp.tanh(half))
+        g = y * zbuf[pl.ds(base, GROUP), :].astype(F32)
         xbuf[pl.ds(HALO + base, GROUP), :] = g.astype(BF16)
         g_copy(i).start()
         squares = (g * g).astype(BF16)
@@ -619,33 +643,29 @@
         def _():
             sums_start(0)
 
-        @pl.when(i == 17)
-        def _():
-            sums_turn(0)
-
     loop(BLOCKS, phase4)
     sums_start(1)
+    sums_turn(0)
+    sums_turn(1)
     sums_end(0)
-    sums_turn(1)
 
     @pl.when(seq < NSEQ - 1)
     def _():
         halo_bc().wait_send()
         halo_x().wait_send()
 
-    def finish(c):
-        for r in order:
-            z_send(c, r).wait_send()
-        y_up(c, my_y).wait_send()
-        y_down(c, my_y).wait_send()
-        f_up(c, below).wait_send()
-        f_down(c, above).wait_send()
-
-    loop(SIDE, finish)
-    for r in (1, 3, 2):
-        side_send(r).wait_send()
-    for hop in range(NZ // 2):
-        ring_done(hop)
+    for kind in range(2):
+        for c in range(len(SPANS)):
+            for r in order:
+                z_send(kind, c, r).wait_send()
+            y_copy(kind, c, my_y, True).wait_send()
+            y_copy(kind, c, my_y, False).wait_send()
+            f_copy(kind, c, below, True).wait_send()
+            f_copy(kind, c, above, False).wait_send()
+        for r in y_order:
+            side_send(kind, r).wait_send()
+        for hop in range(NZ // 2):
+            ring_done(kind, hop)
     others(NSEQ, seq, lambda j: st_copy(j, seq).wait_send())
     others(NSEQ, seq, lambda j: cb_copy(j, seq).wait_send())
 
@@ -706,9 +726,9 @@
             pltpu.VMEM((LENGTH, WIDTH), BF16),
             pltpu.VMEM((BLOCKS, HEADS, HALF, HALF), BF16),
             pltpu.VMEM((BLOCKS, HEADS, HALF, GROUP), BF16),
-            pltpu.VMEM((CHUNKS, NY, NZ, 16, HALF * PER), BF16),
+            pltpu.VMEM((2, NY, NZ, 16, HALF * PAIRS), BF16),
             pltpu.VMEM((BLOCKS, GROUP, STATE), BF16),
-            pltpu.VMEM((BLOCKS, GROUP, GROUP), BF16),
+            pltpu.VMEM((BLOCKS, STATE, GROUP), BF16),
             pltpu.VMEM((LENGTH, WIDTH), F32),
             pltpu.VMEM((BLOCKS, STATE, WIDTH), F32),
             pltpu.VMEM((BLOCKS, GROUP, 24), F32),
@@ -726,25 +746,25 @@
             pltpu.VMEM((NZ, 24, GROUP), F32),
             pltpu.VMEM((24, GROUP), F32),
             pltpu.VMEM((NY, 24, GROUP), F32),
-            dma((CHUNKS,)),
+            dma((LOADS,)),
             dma,
             dma((BLOCKS,)),
             dma((2,)),
             dma((2,)),
-            dma((CHUNKS, NZ)),
-            dma((CHUNKS, NZ)),
-            dma((CHUNKS, 2)),
-            dma((CHUNKS, 2)),
-            dma((CHUNKS, 2)),
-            dma((CHUNKS, 2)),
+            dma((2, len(SPANS), NZ)),
+            dma((2, len(SPANS), NZ)),
+            dma((2, len(SPANS), 2)),
+            dma((2, len(SPANS), 2)),
+            dma((2, len(SPANS), 2)),
+            dma((2, len(SPANS), 2)),
             dma((NSEQ,)),
             dma((NSEQ,)),
             dma((NSEQ,)),
             dma((NSEQ,)),
-            dma((NY,)),
-            dma((NY,)),
-            dma((NZ // 2, 2)),
-            dma((NZ // 2, 2)),
+            dma((2, NY)),
+            dma((2, NY)),
+            dma((2, NZ // 2, 2)),
+            dma((2, NZ // 2, 2)),
             dma((2, NZ)),
             dma((2, NZ)),
             dma((2, NY)),

time: 91.5 us -> 73.3 us (0.80)
  Pallas kernels: 91.2 us -> 72.5 us
    pallas_call x1, Pallas kernels: 87 us -> 68.4 us  [body(): pl.pallas_call(layer, out_shape=(jax.ShapeDtypeStruct((LENGTH, WIDTH), BF...]
where the time goes in v3:
time: 73.3 us; the launch traced here: 72.5 us
  Pallas kernels  72.5 us (99%)
    pallas_call x1, Pallas kernels, body(): pl.pallas_call(layer, out_shape=(jax.ShapeDtypeStruct((LENGTH, WIDTH), BF...  68.4 us
    pallas_call x1, Pallas kernels, body(): pl.pallas_call(scale, out_shape=jax.ShapeDtypeStruct((LENGTH, WIDTH), BF1...  4.13 us

profile of v3, /device:TPU:32, one launch (start us, length us, event | category | flops | bytes accessed | tf_op | source)
XLA Modules:
  0.0 72.5 jit_solution(18387227996774881548)
XLA Ops:
  0.0 68.4 %layer.1 = (bf16[5120,384]{1,0:T(8,128)(2,1)}, f32[24,256]{1,0:T(8,128)}) custom-call(bf16[5120,384]{1,0:T(8,128)(2,1)} %x_hbm.1, bf16[5120,384]{1,0:T(8,128)(2,1)} %z_hbm.1, bf16[4,5120]{1,0:T(4,128)(2,1)} %bitcast.4, bf16[4,5120]{1,0:T(4,128)(2,1)} %bitcast.5, f32[6,5120]{1,0:T(8,128)} %bitcast.3, bf16[4,384]{1,0:T(4,128)(2,1)} %taps_ref.1, ...), custom_call_target="tpu_custom_call" | custom-call | tf_op jit(solution)/shard_map/layer/pallas_call | solution.py:714
  68.4 4.1 %scale.1 = bf16[5120,384]{1,0:T(8,128)(2,1)} custom-call(bf16[5120,384]{1,0:T(8,128)(2,1)} %get-tuple-element.7.g_hbm, f32[24,256]{1,0:T(8,128)} %get-tuple-element.8.total_ref, f32[384]{0:T(512)} %gain_ref.1), custom_call_target="tpu_custom_call" | custom-call | tf_op jit(solution)/shard_map/scale/pallas_call | solution.py:778

commit v4 on v3

--- a/solution.py
+++ b/solution.py
@@ -16,9 +16,10 @@
 PAIRS = BLOCKS // 2
 LOADS = 4
 PER = BLOCKS // LOADS
-SPANS = ((0, 512), (512, 384))
-SIDE = (896, 384)
-SCALED = 4
+FIRST = (0, 128)
+SPANS = (((128, 384), (512, 384)), ((128, 384), (512, 384)))
+SIDE = ((896, 384), (896, 384))
+SCALED = 2
 NSEQ = 8
 NZ = 8
 NY = 4
@@ -64,6 +65,7 @@
     total_ref,
     xbuf,
     zbuf,
+    egate,
     xs_even,
     xs_odd,
     near,
@@ -80,7 +82,8 @@
     bcx,
     prec,
     state,
-    payload,
+    gones,
+    got_decay,
     got,
     back,
     carry_in,
@@ -103,6 +106,12 @@
     st_recv,
     cb_send,
     cb_recv,
+    tz_send,
+    tz_recv,
+    ty_send,
+    ty_recv,
+    sd_send,
+    sd_recv,
     side_out,
     side_in,
     ring_out,
@@ -145,11 +154,6 @@
 
     bcx[0:4, HALF:] = b_ref[...].astype(F32)
     bcx[4:8, HALF:] = c_ref[...].astype(F32)
-    raw = raw_ref[...]
-    stepq[...] = jnp.ones_like(stepq)
-    step_all = jnp.maximum(raw, 0.0) + jnp.log1p(jnp.exp(-jnp.abs(raw)))
-    for i in range(BLOCKS):
-        stepq[i, 0:HEADS, :] = step_all[:, GROUP * i : GROUP * (i + 1)]
     taps_bc = jnp.concatenate([taps_b_ref[...].astype(F32), taps_c_ref[...].astype(F32)], axis=1)
     taps_bc = taps_bc.T * 0.5
     head_row = lax.broadcasted_iota(jnp.int32, (8, GROUP), 0)
@@ -203,13 +207,13 @@
         return gath.at[kind, y, z, :, pl.ds(*span)]
 
     def z_send(kind, c, r):
-        ref = part(kind, my_y, my_z, SPANS[c])
+        ref = part(kind, my_y, my_z, SPANS[kind][c])
         there = lax.rem(my_z + r, NZ) * NY + my_y
         return remote(ref, ref, zs_send.at[kind, c, r], zs_recv.at[kind, c, my_z], head=there)
 
     def z_arrive(kind, c, r):
         other = lax.rem(my_z + r, NZ)
-        ref = part(kind, my_y, other, SPANS[c])
+        ref = part(kind, my_y, other, SPANS[kind][c])
         return remote(
             ref,
             ref,
@@ -221,13 +225,13 @@
     order = (1, 7, 2, 6, 3, 5, 4)
 
     def side_send(kind, r):
-        ref = part(kind, my_y, my_z, SIDE)
+        ref = part(kind, my_y, my_z, SIDE[kind])
         there = my_z * NY + lax.rem(my_y + r, NY)
         return remote(ref, ref, side_out.at[kind, r], side_in.at[kind, my_y], head=there)
 
     def side_arrive(kind, r):
         other = lax.rem(my_y + r, NY)
-        ref = part(kind, other, my_z, SIDE)
+        ref = part(kind, other, my_z, SIDE[kind])
         return remote(
             ref, ref, side_out.at[kind, r], side_in.at[kind, other], head=my_z * NY + other
         )
@@ -238,10 +242,18 @@
         for r in order:
             z_send(kind, c, r).start()
 
+    send_z(0, 0)
     for r in y_order:
         side_send(0, r).start()
     send_z(0, 1)
-
+    for r in y_order:
+        side_send(1, r).start()
+
+    raw = raw_ref[...]
+    stepq[...] = jnp.ones_like(stepq)
+    step_all = jnp.maximum(raw, 0.0) + jnp.log1p(jnp.exp(-jnp.abs(raw)))
+    for i in range(BLOCKS):
+        stepq[i, 0:HEADS, :] = step_all[:, GROUP * i : GROUP * (i + 1)]
     step = stepq[...]
     decay = -(step * rate[None])
     decay = decay.reshape(BLOCKS * 8, GROUP)
@@ -267,7 +279,7 @@
     downs = my_z * NY + below
 
     def y_copy(kind, c, slot, up):
-        ref = gath.at[kind, slot, :, :, pl.ds(*SPANS[c])]
+        ref = gath.at[kind, slot, :, :, pl.ds(*SPANS[kind][c])]
         way = 0 if up else 1
         return remote(
             ref,
@@ -279,7 +291,7 @@
 
     def f_copy(kind, c, slot, up):
         first = 0 if up else NZ // 2
-        ref = gath.at[kind, slot, pl.ds(first, NZ // 2), :, pl.ds(*SPANS[c])]
+        ref = gath.at[kind, slot, pl.ds(first, NZ // 2), :, pl.ds(*SPANS[kind][c])]
         way = 0 if up else 1
         return remote(
             ref,
@@ -295,11 +307,11 @@
     def ring(kind, hop, up, block):
         half = NY // 2
         if hop < NZ // 2 - 1:
-            ref = gath.at[kind, :, block, :, pl.ds(*SIDE)]
+            ref = gath.at[kind, :, block, :, pl.ds(*SIDE[kind])]
         elif up:
-            ref = gath.at[kind, pl.ds(0, half), block, :, pl.ds(*SIDE)]
+            ref = gath.at[kind, pl.ds(0, half), block, :, pl.ds(*SIDE[kind])]
         else:
-            ref = gath.at[kind, pl.ds(half, half), block, :, pl.ds(*SIDE)]
+            ref = gath.at[kind, pl.ds(half, half), block, :, pl.ds(*SIDE[kind])]
         way = 0 if up else 1
         return remote(
             ref,
@@ -346,6 +358,39 @@
         f_copy(kind, c, across, True).wait_recv()
         f_copy(kind, c, across, False).wait_recv()
 
+    def first_part(y, z):
+        return gath.at[:, y, z, :, pl.ds(*FIRST)]
+
+    def first_z(r):
+        ref = first_part(my_y, my_z)
+        there = lax.rem(my_z + r, NZ) * NY + my_y
+        return remote(ref, ref, tz_send.at[r], tz_recv.at[my_z], head=there)
+
+    def first_z_arrive(r):
+        other = lax.rem(my_z + r, NZ)
+        ref = first_part(my_y, other)
+        return remote(ref, ref, tz_send.at[r], tz_recv.at[other], head=other * NY + my_y)
+
+    def first_y(r):
+        ref = gath.at[:, my_y, :, :, pl.ds(*FIRST)]
+        there = my_z * NY + lax.rem(my_y + r, NY)
+        return remote(ref, ref, ty_send.at[r], ty_recv.at[my_y], head=there)
+
+    def first_y_arrive(r):
+        other = lax.rem(my_y + r, NY)
+        ref = gath.at[:, other, :, :, pl.ds(*FIRST)]
+        return remote(ref, ref, ty_send.at[r], ty_recv.at[other], head=my_z * NY + other)
+
+    def event_first():
+        for r in order:
+            first_z_arrive(r).wait_recv()
+        for r in y_order:
+            first_y(r).start()
+
+    def event_first_done():
+        for r in y_order:
+            first_y_arrive(r).wait_recv()
+
     def event_halo():
         @pl.when(seq > 0)
         def _():
@@ -360,38 +405,48 @@
         first = conv_bc(bcx[:, 0 : 2 * HALF])[:, HALF:]
         for kind in range(2):
             put_tile(kind, 0, [first] + quarters[1:4])
-        send_z(0, 0)
-        for r in y_order:
-            side_send(1, r).start()
+        for r in order:
+            first_z(r).start()
 
     taps = taps_ref[...].astype(F32) * 0.5
-    lanes = lax.broadcasted_iota(jnp.int32, (GROUP, WIDTH), 1)
-    even = (lanes & 127) < 64
+    even = lax.broadcasted_iota(jnp.int32, (HALF, HALF), 1) < 64
     row1 = lax.broadcasted_iota(jnp.int32, (HALF, HALF), 0)
     col1 = lax.broadcasted_iota(jnp.int32, (HALF, HALF), 1)
     causal = row1 >= col1
+    of_head = lax.broadcasted_iota(jnp.int32, (8, WIDTH), 1) >> 6
 
     def phase1(i):
         base = pl.multiple_of(i * GROUP, GROUP)
-        wide = xbuf[pl.ds(base, GROUP + HALO), :].astype(F32)
-        once = pltpu.roll(wide, 1, axis=0)
-        older = pltpu.roll(wide * taps[1:2] + once * taps[0:1], 2, axis=0)
-        half = wide[HALO:] * taps[3:4] + once[HALO:] * taps[2:3] + older[HALO:]
-        xs = (half + half * jnp.tanh(half)).astype(BF16)
-        none = jnp.zeros_like(xs)
-        xs_even[pl.ds(base, GROUP), :] = jnp.where(even, xs, none)
-        xs_odd[pl.ds(base, GROUP), :] = jnp.where(even, none, xs)
+        for low in (0, HALF):
+            for lane in range(0, WIDTH, HALF):
+                span = slice(lane, lane + HALF)
+                wide = xbuf[pl.ds(base + low, HALF + HALO), span].astype(F32)
+                once = pltpu.roll(wide, 1, axis=0)
+                older = pltpu.roll(wide * taps[1:2, span] + once * taps[0:1, span], 2, axis=0)
+                half = (
+                    wide[HALO:] * taps[3:4, span] + once[HALO:] * taps[2:3, span] + older[HALO:]
+                )
+                xs = (half + half * jnp.tanh(half)).astype(BF16)
+                none = jnp.zeros_like(xs)
+                xs_even[pl.ds(base + low, HALF), span] = jnp.where(even, xs, none)
+                xs_odd[pl.ds(base + low, HALF), span] = jnp.where(even, none, xs)
         cols = rowq[i].T
         colq[i] = cols
+        ends = cols[GROUP - 8 :, 16:24]
+        gone = jnp.zeros((8, WIDTH), F32)
+        for h in range(HEADS):
+            gone = jnp.where(of_head == h, ends[7:8, h : h + 1], gone)
+        gones[i] = gone
         b_all = bq[i]
         for h in range(HEADS):
             a = cols[:, h : h + 1]
             b = b_all[h : h + 1, :]
-            near[i, h] = jnp.exp(jnp.where(causal, a[:HALF] - b[:, :HALF], MASKED)).astype(BF16)
-            far[i, h, :, 0:HALF] = jnp.exp(a[HALF:] - b[:, :HALF]).astype(BF16)
-            far[i, h, :, HALF:] = jnp.exp(
-                jnp.where(causal, a[HALF:] - b[:, HALF:], MASKED)
-            ).astype(BF16)
+            gap1 = jnp.where(causal, a[:HALF] - b[:, :HALF], MASKED)
+            gap2 = a[HALF:] - b[:, :HALF]
+            gap3 = jnp.where(causal, a[HALF:] - b[:, HALF:], MASKED)
+            near[i, h] = jnp.exp(gap1.astype(BF16))
+            far[i, h, :, 0:HALF] = jnp.exp(gap2.astype(BF16))
+            far[i, h, :, HALF:] = jnp.exp(gap3.astype(BF16))
 
     def step1(i):
         block = lax.rem(i + 1, BLOCKS)
@@ -402,34 +457,56 @@
 
         phase1(block)
 
-        for when, events in during.items():
-
-            @pl.when(i == when)
-            def _(events=events):
-                for event, *which in events:
-                    event(*which)
-
-    during = {
-        4: [(event_halo,)],
-        5: [(event_side, 0)],
-        7: [(event_z, 0, 1), (send_z, 1, 1)],
-        11: [(event_ring, 0, 1)],
-        12: [(event_z, 0, 0)],
-        14: [(event_f, 0, 1)],
-        16: [(event_ring, 0, 2), (send_z, 1, 0)],
-        17: [(event_side, 1)],
-    }
-    loop(BLOCKS, step1)
+    def run(count, unit, before):
+        def step(i):
+            for when, events in before.items():
+
+                @pl.when(i == when)
+                def _(events=events):
+                    for event, *which in events:
+                        event(*which)
+
+            unit(i)
+
+        loop(count, step)
+
+    run(
+        BLOCKS,
+        step1,
+        {
+            5: [(event_side, 0), (event_side, 1), (event_halo,), (send_z, 1, 0)],
+            9: [(event_z, 0, 0)],
+            12: [(event_ring, 0, 1), (event_z, 0, 1), (send_z, 1, 1)],
+            14: [(event_ring, 1, 1), (event_first,)],
+            15: [(event_f, 0, 0)],
+            18: [(event_f, 0, 1), (event_ring, 0, 2)],
+        },
+    )
 
     spread_row = lax.broadcasted_iota(jnp.int32, (24, WIDTH), 0)
     spread_col = lax.broadcasted_iota(jnp.int32, (24, WIDTH), 1) >> 6
     spread_w = jnp.where(spread_row == spread_col + 8, 1.0, 0.0).astype(BF16)
     spread_e = jnp.where(spread_row == spread_col + 16, 1.0, 0.0).astype(BF16)
-    of_head = lax.broadcasted_iota(jnp.int32, (8, WIDTH), 1) >> 6
     upper4 = lax.broadcasted_iota(jnp.int32, (8, HALF), 0) < 4
 
     state[...] = jnp.zeros_like(state)
-    prec[0] = jnp.ones((8, WIDTH), F32)
+
+    so_far = jnp.ones((8, WIDTH), F32)
+    prec[0] = so_far
+    for i in range(BLOCKS):
+        so_far = so_far * gones[i]
+        prec[i + 1] = so_far
+    got_decay[seq] = so_far
+
+    def others(count, me, body):
+        loop(count - 1, lambda r: body(lax.rem(me + 1 + r, count)))
+
+    def sd_copy(j, slot):
+        return remote(
+            prec.at[BLOCKS], got_decay.at[slot], sd_send.at[j], sd_recv.at[slot], seq=j
+        )
+
+    others(NSEQ, seq, lambda j: sd_copy(j, seq).start())
 
     def assemble(kind, j):
         lane = pl.multiple_of(j * HALF, HALF)
@@ -447,6 +524,7 @@
         return [jnp.concatenate(block, axis=0) for block in blocks]
 
     def phase2(j):
+        news, goes = [], []
         for e, b_t in enumerate(assemble(0, j)):
             i = 2 * j + e
             b_t = b_t.astype(BF16)
@@ -455,15 +533,13 @@
             xs = (xs_even[pl.ds(base, GROUP), :] + xs_odd[pl.ds(base, GROUP), :]).astype(F32)
             cols = colq[i]
             weight = dot(cols.astype(BF16), spread_w)
-            new = dot(b_t, (weight * xs).astype(BF16))
-            ends = cols[GROUP - 8 :, 16:24]
-            gone = jnp.zeros((8, WIDTH), F32)
-            for h in range(HEADS):
-                gone = jnp.where(of_head == h, ends[7:8, h : h + 1], gone)
-            old = state[...]
-            local_state[i] = old
-            state[...] = old * gone[0:1] + new
-            prec[i + 1] = prec[i] * gone
+            news.append(dot(b_t, (weight * xs).astype(BF16)))
+            goes.append(gones[i])
+        old = state[...]
+        local_state[2 * j] = old
+        old = old * goes[0][0:1] + news[0]
+        local_state[2 * j + 1] = old
+        state[...] = old * goes[1][0:1] + news[1]
 
     def phase3(j):
         for e, c_t in enumerate(assemble(1, j)):
@@ -482,41 +558,44 @@
                     [top * near[i, 2 * pair], top * near[i, 2 * pair + 1]], axis=1
                 )
                 x1 = jnp.concatenate([xe[:HALF], xo[:HALF]], axis=0)
-                ydiag[pl.ds(base, HALF), span] = dot(m1, x1)
+                gate1 = zbuf[pl.ds(base, HALF), span].astype(F32)
+                ydiag[pl.ds(base, HALF), span] = dot(m1, x1) * gate1
                 m2 = jnp.concatenate(
                     [low_rows * far[i, 2 * pair], low_rows * far[i, 2 * pair + 1]], axis=1
                 )
                 x2 = jnp.concatenate([xe, xo], axis=0)
-                ydiag[pl.ds(base + HALF, HALF), span] = dot(m2, x2)
+                gate2 = zbuf[pl.ds(base + HALF, HALF), span].astype(F32)
+                ydiag[pl.ds(base + HALF, HALF), span] = dot(m2, x2) * gate2
 
     def gates(i):
         base = pl.multiple_of(i * GROUP, GROUP)
         half = zbuf[pl.ds(base, GROUP), :].astype(F32) * 0.5
-        zbuf[pl.ds(base, GROUP), :] = (half + half * jnp.tanh(half)).astype(BF16)
-
-    event_f(0, 0)
-    event_z(1, 1)
+        gate = half + half * jnp.tanh(half)
+        zbuf[pl.ds(base, GROUP), :] = gate.astype(BF16)
+        grown = dot(colq[i].astype(BF16), spread_e)
+        egate[pl.ds(base, GROUP), :] = (gate * grown).astype(BF16)
+
     z_copy.wait()
-    loop(BLOCKS // 2, gates)
-    event_ring(0, 3)
-    loop(BLOCKS // 2, lambda i: gates(BLOCKS // 2 + i))
-    event_ring(1, 1)
-    event_d(0, 0)
-    loop(4, phase2)
-    event_z(1, 0)
-    event_d(0, 1)
-    loop(3, lambda j: phase2(4 + j))
-    event_f(1, 1)
-    event_ring(1, 2)
-    ring_arrive(0, 3)
-    loop(3, lambda j: phase2(7 + j))
-
-    for j in range(NSEQ):
-        payload[j, 0:PART, :] = state[PART * j : PART * (j + 1), :]
-        payload[j, PART : PART + 8, :] = prec[BLOCKS]
+    run(BLOCKS // 2, gates, {0: [(event_z, 1, 0)]})
+    run(
+        PAIRS,
+        phase2,
+        {
+            0: [(event_ring, 1, 2), (event_first_done,)],
+            1: [(event_d, 0, 0)],
+            2: [(event_ring, 0, 3), (event_z, 1, 1)],
+            4: [(event_d, 0, 1)],
+            6: [(event_ring, 1, 3)],
+            7: [(ring_arrive, 0, 3)],
+            8: [(event_f, 1, 0)],
+        },
+    )
 
     def st_copy(j, slot):
-        return remote(payload.at[j], got.at[slot], st_send.at[j], st_recv.at[slot], seq=j)
+        place = pl.multiple_of(j * PART, PART)
+        return remote(
+            state.at[pl.ds(place, PART)], got.at[slot], st_send.at[j], st_recv.at[slot], seq=j
+        )
 
     def cb_copy(j, slot):
         place = pl.multiple_of(slot * PART, PART)
@@ -524,26 +603,29 @@
             back.at[j], carry_in.at[pl.ds(place, PART)], cb_send.at[j], cb_recv.at[slot], seq=j
         )
 
-    def others(count, me, body):
-        loop(count - 1, lambda r: body(lax.rem(me + 1 + r, count)))
-
     others(NSEQ, seq, lambda j: st_copy(j, seq).start())
-    got[seq] = payload[seq]
-    event_f(1, 0)
-    event_ring(1, 3)
-    event_d(1, 1)
-    loop(3, lambda j: phase3(4 + j))
-    others(NSEQ, seq, lambda j: st_copy(j, j).wait_recv())
-    carry = jnp.zeros((PART, WIDTH), F32)
-    for j in range(NSEQ):
-        back[j] = carry
-        carry = carry * got[j, PART : PART + 1, :] + got[j, 0:PART, :]
-    others(NSEQ, seq, lambda j: cb_copy(j, seq).start())
-    carry_in[pl.ds(pl.multiple_of(seq * PART, PART), PART), :] = back[seq]
-    event_d(1, 0)
-    loop(4, phase3)
-    ring_arrive(1, 3)
-    loop(3, lambda j: phase3(7 + j))
+    got[seq] = state[pl.ds(pl.multiple_of(seq * PART, PART), PART), :]
+    run(BLOCKS // 2, lambda i: gates(BLOCKS // 2 + i), {6: [(event_f, 1, 1)]})
+
+    def event_states():
+        others(NSEQ, seq, lambda j: sd_copy(j, j).wait_recv())
+        others(NSEQ, seq, lambda j: st_copy(j, j).wait_recv())
+        carry = jnp.zeros((PART, WIDTH), F32)
+        for j in range(NSEQ):
+            back[j] = carry
+            carry = carry * got_decay[j, 0:1, :] + got[j]
+        others(NSEQ, seq, lambda j: cb_copy(j, seq).start())
+        carry_in[pl.ds(pl.multiple_of(seq * PART, PART), PART), :] = back[seq]
+
+    run(
+        PAIRS,
+        lambda i: phase3(lax.rem(i + 7, PAIRS)),
+        {
+            0: [(ring_arrive, 1, 3)],
+            4: [(event_d, 1, 0), (event_states,)],
+            7: [(event_d, 1, 1)],
+        },
+    )
     others(NSEQ, seq, lambda j: cb_copy(j, j).wait_recv())
 
     ones = jnp.ones((8, WIDTH), BF16)
@@ -620,30 +702,34 @@
             added = added + sums_y[k, parts[p], :]
         total_ref[parts[p], :] = added
 
-    def phase4(i):
-        base = pl.multiple_of(i * GROUP, GROUP)
-        whole = local_state[i] + carry_in[...] * prec[i][0:1]
-        whole_high = whole.astype(BF16)
-        whole_low = (whole - whole_high.astype(F32)).astype(BF16)
-        c_i = cmat[i]
-        carried = dot(
-            jnp.concatenate([c_i, c_i], axis=1),
-            jnp.concatenate([whole_high, whole_low], axis=0),
-        )
-        grown = dot(colq[i].astype(BF16), spread_e)
-        y = ydiag[pl.ds(base, GROUP), :] + carried * grown
-        g = y * zbuf[pl.ds(base, GROUP), :].astype(F32)
-        xbuf[pl.ds(HALO + base, GROUP), :] = g.astype(BF16)
-        g_copy(i).start()
-        squares = (g * g).astype(BF16)
-        sums = lax.dot_general(ones, squares, (((1,), (1,)), ((), ())), preferred_element_type=F32)
-        sums_row[pl.ds(jnp.where(i < 12, i, i + 4), 1), :] = sums[0:1]
-
-        @pl.when(i == 11)
+    def phase4(j):
+        for e in range(2):
+            i = 2 * j + e
+            base = pl.multiple_of(i * GROUP, GROUP)
+            whole = local_state[i] + carry_in[...] * prec[i][0:1]
+            whole_high = whole.astype(BF16)
+            whole_low = (whole - whole_high.astype(F32)).astype(BF16)
+            c_i = cmat[i]
+            carried = dot(
+                jnp.concatenate([c_i, c_i], axis=1),
+                jnp.concatenate([whole_high, whole_low], axis=0),
+            )
+            g = ydiag[pl.ds(base, GROUP), :] + carried * egate[pl.ds(base, GROUP), :].astype(F32)
+            g = g.astype(BF16)
+            xbuf[pl.ds(HALO + base, GROUP), :] = g
+            squares = g * g
+            sums = lax.dot_general(
+                ones, squares, (((1,), (1,)), ((), ())), preferred_element_type=F32
+            )
+            sums_row[pl.ds(jnp.where(i < 12, i, i + 4), 1), :] = sums[0:1]
+        g_copy(2 * j).start()
+        g_copy(2 * j + 1).start()
+
+        @pl.when(j == 5)
         def _():
             sums_start(0)
 
-    loop(BLOCKS, phase4)
+    loop(PAIRS, phase4)
     sums_start(1)
     sums_turn(0)
     sums_turn(1)
@@ -654,8 +740,13 @@
         halo_bc().wait_send()
         halo_x().wait_send()
 
+    for r in order:
+        first_z(r).wait_send()
+    for r in y_order:
+        first_y(r).wait_send()
+    others(NSEQ, seq, lambda j: sd_copy(j, seq).wait_send())
     for kind in range(2):
-        for c in range(len(SPANS)):
+        for c in range(2):
             for r in order:
                 z_send(kind, c, r).wait_send()
             y_copy(kind, c, my_y, True).wait_send()
@@ -679,7 +770,7 @@
             sy_copy(p, r).wait_send()
 
 
-def scale(g_hbm, total_ref, gain_ref, out_hbm, g_in, g_out, in_sem, out_sem):
+def scale(g_hbm, total_hbm, gain_hbm, out_hbm, g_in, g_out, total, gain_in, in_sem, out_sem, sem):
     rows = GROUP * SCALED
 
     def come(k):
@@ -690,10 +781,16 @@
         part = pl.ds(rows * k, rows)
         return pltpu.make_async_copy(g_out.at[part], out_hbm.at[part], out_sem.at[k])
 
+    total_copy = pltpu.make_async_copy(total_hbm, total, sem.at[0])
+    gain_copy = pltpu.make_async_copy(gain_hbm, gain_in, sem.at[1])
+    total_copy.start()
+    gain_copy.start()
     for k in range(BLOCKS // SCALED):
         come(k).start()
-    gain = gain_ref[...][None, :]
-    factor = lax.rsqrt(total_ref[...] * (1.0 / (NHEAD * WIDTH)) + 1e-05).T
+    total_copy.wait()
+    gain_copy.wait()
+    gain = gain_in[...][None, :]
+    factor = lax.rsqrt(total[...] * (1.0 / (NHEAD * WIDTH)) + 1e-05).T
     for k in range(BLOCKS // SCALED):
         come(k).wait()
         for j in range(SCALED * k, SCALED * (k + 1)):
@@ -724,6 +821,7 @@
             pltpu.VMEM((LENGTH, WIDTH), BF16),
             pltpu.VMEM((LENGTH, WIDTH), BF16),
             pltpu.VMEM((LENGTH, WIDTH), BF16),
+            pltpu.VMEM((LENGTH, WIDTH), BF16),
             pltpu.VMEM((BLOCKS, HEADS, HALF, HALF), BF16),
             pltpu.VMEM((BLOCKS, HEADS, HALF, GROUP), BF16),
             pltpu.VMEM((2, NY, NZ, 16, HALF * PAIRS), BF16),
@@ -738,8 +836,9 @@
             pltpu.VMEM((8, HALF + LENGTH), F32),
             pltpu.VMEM((BLOCKS + 1, 8, WIDTH), F32),
             pltpu.VMEM((STATE, WIDTH), F32),
-            pltpu.VMEM((NSEQ, PART + 8, WIDTH), F32),
-            pltpu.VMEM((NSEQ, PART + 8, WIDTH), F32),
+            pltpu.VMEM((BLOCKS, 8, WIDTH), F32),
+            pltpu.VMEM((NSEQ, 8, WIDTH), F32),
+            pltpu.VMEM((NSEQ, PART, WIDTH), F32),
             pltpu.VMEM((NSEQ, PART, WIDTH), F32),
             pltpu.VMEM((STATE, WIDTH), F32),
             pltpu.VMEM((24, GROUP), F32),
@@ -751,14 +850,20 @@
             dma((BLOCKS,)),
             dma((2,)),
             dma((2,)),
-            dma((2, len(SPANS), NZ)),
-            dma((2, len(SPANS), NZ)),
-            dma((2, len(SPANS), 2)),
-            dma((2, len(SPANS), 2)),
-            dma((2, len(SPANS), 2)),
-            dma((2, len(SPANS), 2)),
+            dma((2, 2, NZ)),
+            dma((2, 2, NZ)),
+            dma((2, 2, 2)),
+            dma((2, 2, 2)),
+            dma((2, 2, 2)),
+            dma((2, 2, 2)),
             dma((NSEQ,)),
             dma((NSEQ,)),
+            dma((NSEQ,)),
+            dma((NSEQ,)),
+            dma((NZ,)),
+            dma((NZ,)),
+            dma((NY,)),
+            dma((NY,)),
             dma((NSEQ,)),
             dma((NSEQ,)),
             dma((2, NY)),
@@ -778,13 +883,16 @@
     return pl.pallas_call(
         scale,
         out_shape=jax.ShapeDtypeStruct((LENGTH, WIDTH), BF16),
-        in_specs=[hbm, vmem, vmem],
+        in_specs=[hbm, hbm, hbm],
         out_specs=hbm,
         scratch_shapes=[
             pltpu.VMEM((LENGTH, WIDTH), BF16),
             pltpu.VMEM((LENGTH, WIDTH), BF16),
+            pltpu.VMEM((24, GROUP), F32),
+            pltpu.VMEM((WIDTH,), F32),
             dma((BLOCKS // SCALED,)),
             dma((BLOCKS // SCALED,)),
+            dma((2,)),
         ],
         compiler_params=pltpu.CompilerParams(vmem_limit_bytes=60 * 2**20),
         name="scale",

time: 73.3 us -> 69.6 us (0.950)
  Pallas kernels: 72.5 us -> 68.7 us
    pallas_call x1, Pallas kernels: 68.4 us -> 64.4 us  [body(): pl.pallas_call(layer, out_shape=(jax.ShapeDtypeStruct((LENGTH, WIDTH), BF...]
where the time goes in v4:
time: 69.6 us; the launch traced here: 68.7 us
  Pallas kernels  68.7 us (99%)
    pallas_call x1, Pallas kernels, body(): pl.pallas_call(layer, out_shape=(jax.ShapeDtypeStruct((LENGTH, WIDTH), BF...  64.4 us
    pallas_call x1, Pallas kernels, body(): pl.pallas_call(scale, out_shape=jax.ShapeDtypeStruct((LENGTH, WIDTH), BF1...  4.35 us

profile of v4, /device:TPU:32, one launch (start us, length us, event | category | flops | bytes accessed | tf_op | source)
XLA Modules:
  0.0 68.7 jit_solution(16167245306272061467)
XLA Ops:
  0.0 64.4 %layer.1 = (bf16[5120,384]{1,0:T(8,128)(2,1)}, f32[24,256]{1,0:T(8,128)}) custom-call(bf16[5120,384]{1,0:T(8,128)(2,1)} %x_hbm.1, bf16[5120,384]{1,0:T(8,128)(2,1)} %z_hbm.1, bf16[4,5120]{1,0:T(4,128)(2,1)} %bitcast.4, bf16[4,5120]{1,0:T(4,128)(2,1)} %bitcast.5, f32[6,5120]{1,0:T(8,128)} %bitcast.3, bf16[4,384]{1,0:T(4,128)(2,1)} %taps_ref.1, ...), custom_call_target="tpu_custom_call" | custom-call | tf_op jit(solution)/shard_map/layer/pallas_call | solution.py:811
  64.4 4.3 %scale.1 = bf16[5120,384]{1,0:T(8,128)(2,1)} custom-call(bf16[5120,384]{1,0:T(8,128)(2,1)} %get-tuple-element.7.g_hbm, f32[24,256]{1,0:T(8,128)} %get-tuple-element.8.total_hbm, f32[384]{0:T(512)} %gain_hbm.1), custom_call_target="tpu_custom_call" | custom-call | tf_op jit(solution)/shard_map/scale/pallas_call | solution.py:883

commit v5 on v4

--- a/solution.py
+++ b/solution.py
@@ -524,17 +524,18 @@
         return [jnp.concatenate(block, axis=0) for block in blocks]
 
     def phase2(j):
-        news, goes = [], []
-        for e, b_t in enumerate(assemble(0, j)):
-            i = 2 * j + e
-            b_t = b_t.astype(BF16)
+        blocks = (2 * j, 2 * j + 1)
+        bases = [pl.multiple_of(i * GROUP, GROUP) for i in blocks]
+        weights = [dot(colq[i].astype(BF16), spread_w) for i in blocks]
+        b_ts = [b_t.astype(BF16) for b_t in assemble(0, j)]
+        weighted = []
+        for base, weight in zip(bases, weights):
+            xs = (xs_even[pl.ds(base, GROUP), :] + xs_odd[pl.ds(base, GROUP), :]).astype(F32)
+            weighted.append((weight * xs).astype(BF16))
+        news = [dot(b_t, w) for b_t, w in zip(b_ts, weighted)]
+        for i, b_t in zip(blocks, b_ts):
             bmat[i] = b_t
-            base = pl.multiple_of(i * GROUP, GROUP)
-            xs = (xs_even[pl.ds(base, GROUP), :] + xs_odd[pl.ds(base, GROUP), :]).astype(F32)
-            cols = colq[i]
-            weight = dot(cols.astype(BF16), spread_w)
-            news.append(dot(b_t, (weight * xs).astype(BF16)))
-            goes.append(gones[i])
+        goes = [gones[i] for i in blocks]
         old = state[...]
         local_state[2 * j] = old
         old = old * goes[0][0:1] + news[0]
@@ -542,30 +543,33 @@
         state[...] = old * goes[1][0:1] + news[1]
 
     def phase3(j):
-        for e, c_t in enumerate(assemble(1, j)):
-            i = 2 * j + e
-            c_i = c_t.T.astype(BF16)
+        blocks = (2 * j, 2 * j + 1)
+        bases = [pl.multiple_of(i * GROUP, GROUP) for i in blocks]
+        c_is = [c_t.T.astype(BF16) for c_t in assemble(1, j)]
+        scores = [dot(c_i, bmat[i]).astype(BF16) for i, c_i in zip(blocks, c_is)]
+        for i, c_i in zip(blocks, c_is):
             cmat[i] = c_i
-            base = pl.multiple_of(i * GROUP, GROUP)
-            scores = dot(c_i, bmat[i]).astype(BF16)
-            top = scores[:HALF, :HALF]
-            low_rows = scores[HALF:, :]
-            for pair in range(HEADS // 2):
-                span = slice(HALF * pair, HALF * (pair + 1))
+        for pair in range(HEADS // 2):
+            span = slice(HALF * pair, HALF * (pair + 1))
+            results = []
+            for i, base, score in zip(blocks, bases, scores):
+                top = score[:HALF, :HALF]
+                low_rows = score[HALF:, :]
                 xe = xs_even[pl.ds(base, GROUP), span]
                 xo = xs_odd[pl.ds(base, GROUP), span]
                 m1 = jnp.concatenate(
                     [top * near[i, 2 * pair], top * near[i, 2 * pair + 1]], axis=1
                 )
-                x1 = jnp.concatenate([xe[:HALF], xo[:HALF]], axis=0)
-                gate1 = zbuf[pl.ds(base, HALF), span].astype(F32)
-                ydiag[pl.ds(base, HALF), span] = dot(m1, x1) * gate1
                 m2 = jnp.concatenate(
                     [low_rows * far[i, 2 * pair], low_rows * far[i, 2 * pair + 1]], axis=1
                 )
+                x1 = jnp.concatenate([xe[:HALF], xo[:HALF]], axis=0)
                 x2 = jnp.concatenate([xe, xo], axis=0)
-                gate2 = zbuf[pl.ds(base + HALF, HALF), span].astype(F32)
-                ydiag[pl.ds(base + HALF, HALF), span] = dot(m2, x2) * gate2
+                results.append((dot(m1, x1), dot(m2, x2)))
+            for base, (upper_rows, lower_rows) in zip(bases, results):
+                gate = zbuf[pl.ds(base, GROUP), span].astype(F32)
+                ydiag[pl.ds(base, HALF), span] = upper_rows * gate[:HALF]
+                ydiag[pl.ds(base + HALF, HALF), span] = lower_rows * gate[HALF:]
 
     def gates(i):
         base = pl.multiple_of(i * GROUP, GROUP)
@@ -703,33 +707,36 @@
         total_ref[parts[p], :] = added
 
     def phase4(j):
-        for e in range(2):
-            i = 2 * j + e
-            base = pl.multiple_of(i * GROUP, GROUP)
+        blocks = [4 * j + e for e in range(4)]
+        bases = [pl.multiple_of(i * GROUP, GROUP) for i in blocks]
+        operands = []
+        for i in blocks:
             whole = local_state[i] + carry_in[...] * prec[i][0:1]
             whole_high = whole.astype(BF16)
             whole_low = (whole - whole_high.astype(F32)).astype(BF16)
+            operands.append(jnp.concatenate([whole_high, whole_low], axis=0))
+        products = []
+        for i, operand in zip(blocks, operands):
             c_i = cmat[i]
-            carried = dot(
-                jnp.concatenate([c_i, c_i], axis=1),
-                jnp.concatenate([whole_high, whole_low], axis=0),
+            products.append(dot(jnp.concatenate([c_i, c_i], axis=1), operand))
+        values = []
+        for base, carried in zip(bases, products):
+            factor = egate[pl.ds(base, GROUP), :].astype(F32)
+            values.append((ydiag[pl.ds(base, GROUP), :] + carried * factor).astype(BF16))
+        for i, base, g in zip(blocks, bases, values):
+            sums = lax.dot_general(
+                ones, g * g, (((1,), (1,)), ((), ())), preferred_element_type=F32
             )
-            g = ydiag[pl.ds(base, GROUP), :] + carried * egate[pl.ds(base, GROUP), :].astype(F32)
-            g = g.astype(BF16)
             xbuf[pl.ds(HALO + base, GROUP), :] = g
-            squares = g * g
-            sums = lax.dot_general(
-                ones, squares, (((1,), (1,)), ((), ())), preferred_element_type=F32
-            )
             sums_row[pl.ds(jnp.where(i < 12, i, i + 4), 1), :] = sums[0:1]
-        g_copy(2 * j).start()
-        g_copy(2 * j + 1).start()
-
-        @pl.when(j == 5)
+        for i in blocks:
+            g_copy(i).start()
+
+        @pl.when(j == 2)
         def _():
             sums_start(0)
 
-    loop(PAIRS, phase4)
+    loop(BLOCKS // 4, phase4)
     sums_start(1)
     sums_turn(0)
     sums_turn(1)
@@ -796,8 +803,7 @@
         for j in range(SCALED * k, SCALED * (k + 1)):
             place = j if j < 12 else j + 4
             part = slice(GROUP * j, GROUP * (j + 1))
-            scaled = g_in[part, :].astype(F32) * factor[:, place : place + 1] * gain
-            g_out[part, :] = scaled.astype(BF16)
+            g_out[part, :] = g_in[part, :] * (factor[:, place : place + 1] * gain).astype(BF16)
         go(k).start()
     for k in range(BLOCKS // SCALED):
         go(k).wait()

time: 69.6 us -> 66 us (0.948); the launches traced: 68.7 us -> 65.9 us
  Pallas kernels: 68.7 us -> 65.9 us
    pallas_call x1, Pallas kernels: 64.4 us -> 61.7 us  [body(): pl.pallas_call(layer, out_shape=(jax.ShapeDtypeStruct((LENGTH, WIDTH), BF...]
where the time goes in v5:
time: 66 us; the launch traced here: 65.9 us
  Pallas kernels  65.9 us (100%)
    pallas_call x1, Pallas kernels, body(): pl.pallas_call(layer, out_shape=(jax.ShapeDtypeStruct((LENGTH, WIDTH), BF...  61.7 us
    pallas_call x1, Pallas kernels, body(): pl.pallas_call(scale, out_shape=jax.ShapeDtypeStruct((LENGTH, WIDTH), BF1...  4.21 us

profile of v5, /device:TPU:32, one launch (start us, length us, event | category | flops | bytes accessed | tf_op | source)
XLA Modules:
  0.0 65.9 jit_solution(72335269069934374)
XLA Ops:
  0.0 61.7 %layer.1 = (bf16[5120,384]{1,0:T(8,128)(2,1)}, f32[24,256]{1,0:T(8,128)}) custom-call(bf16[5120,384]{1,0:T(8,128)(2,1)} %x_hbm.1, bf16[5120,384]{1,0:T(8,128)(2,1)} %z_hbm.1, bf16[4,5120]{1,0:T(4,128)(2,1)} %bitcast.4, bf16[4,5120]{1,0:T(4,128)(2,1)} %bitcast.5, f32[6,5120]{1,0:T(8,128)} %bitcast.3, bf16[4,384]{1,0:T(4,128)(2,1)} %taps_ref.1, ...), custom_call_target="tpu_custom_call" | custom-call | tf_op jit(solution)/shard_map/layer/pallas_call | solution.py:817
  61.7 4.2 %scale.1 = bf16[5120,384]{1,0:T(8,128)(2,1)} custom-call(bf16[5120,384]{1,0:T(8,128)(2,1)} %get-tuple-element.7.g_hbm, f32[24,256]{1,0:T(8,128)} %get-tuple-element.8.total_hbm, f32[384]{0:T(512)} %gain_hbm.1), custom_call_target="tpu_custom_call" | custom-call | tf_op jit(solution)/shard_map/scale/pallas_call | solution.py:889

commit v6 on v5

--- a/solution.py
+++ b/solution.py
@@ -267,9 +267,13 @@
     cum = dot(high, upper) + (dot(mid, upper) + dot(low, upper))
     last = cum[:, GROUP - 1 : GROUP]
     step2 = step.reshape(BLOCKS * 8, GROUP)
-    rowq[:, 0:8, :] = cum.reshape(BLOCKS, 8, GROUP)
-    rowq[:, 8:16, :] = (jnp.exp(last - cum) * step2).reshape(BLOCKS, 8, GROUP)
-    rowq[:, 16:24, :] = jnp.exp(cum).reshape(BLOCKS, 8, GROUP)
+    cum_high = cum.astype(BF16).astype(F32)
+    cum_mid = (cum - cum_high).astype(BF16).astype(F32)
+    rowq[:, 0:8, :] = cum_high.reshape(BLOCKS, 8, GROUP)
+    rowq[:, 8:16, :] = cum_mid.reshape(BLOCKS, 8, GROUP)
+    rowq[:, 16:24, :] = (cum - cum_high - cum_mid).reshape(BLOCKS, 8, GROUP)
+    rowq[:, 24:32, :] = (jnp.exp(last - cum) * step2).reshape(BLOCKS, 8, GROUP)
+    rowq[:, 32:40, :] = jnp.exp(cum).reshape(BLOCKS, 8, GROUP)
     bq[...] = (cum - jnp.log(step2)).reshape(BLOCKS, 8, GROUP)
 
     above = lax.rem(my_y + 1, NY)
@@ -413,6 +417,10 @@
     row1 = lax.broadcasted_iota(jnp.int32, (HALF, HALF), 0)
     col1 = lax.broadcasted_iota(jnp.int32, (HALF, HALF), 1)
     causal = row1 >= col1
+    spread_row = lax.broadcasted_iota(jnp.int32, (40, HALF * HEADS), 0)
+    spread_col = lax.broadcasted_iota(jnp.int32, (40, HALF * HEADS), 1) >> 7
+    picked = (spread_row < 24) & ((spread_row & 7) == spread_col)
+    spread_a = jnp.where(picked, 1.0, 0.0).astype(BF16)
     of_head = lax.broadcasted_iota(jnp.int32, (8, WIDTH), 1) >> 6
 
     def phase1(i):
@@ -431,15 +439,18 @@
                 xs_even[pl.ds(base + low, HALF), span] = jnp.where(even, xs, none)
                 xs_odd[pl.ds(base + low, HALF), span] = jnp.where(even, none, xs)
         cols = rowq[i].T
-        colq[i] = cols
-        ends = cols[GROUP - 8 :, 16:24]
+        colb = cols.astype(BF16)
+        colq[i] = colb
+        ends = cols[GROUP - 8 :, 32:40]
         gone = jnp.zeros((8, WIDTH), F32)
         for h in range(HEADS):
             gone = jnp.where(of_head == h, ends[7:8, h : h + 1], gone)
         gones[i] = gone
         b_all = bq[i]
         for h in range(HEADS):
-            a = cols[:, h : h + 1]
+            if h % 2 == 0:
+                two = dot(colb, spread_a[:, HALF * h : HALF * (h + 2)])
+            a = two[:, HALF * (h % 2) : HALF * (h % 2 + 1)]
             b = b_all[h : h + 1, :]
             gap1 = jnp.where(causal, a[:HALF] - b[:, :HALF], MASKED)
             gap2 = a[HALF:] - b[:, :HALF]
@@ -483,10 +494,10 @@
         },
     )
 
-    spread_row = lax.broadcasted_iota(jnp.int32, (24, WIDTH), 0)
-    spread_col = lax.broadcasted_iota(jnp.int32, (24, WIDTH), 1) >> 6
-    spread_w = jnp.where(spread_row == spread_col + 8, 1.0, 0.0).astype(BF16)
-    spread_e = jnp.where(spread_row == spread_col + 16, 1.0, 0.0).astype(BF16)
+    spread_row = lax.broadcasted_iota(jnp.int32, (40, WIDTH), 0)
+    spread_col = lax.broadcasted_iota(jnp.int32, (40, WIDTH), 1) >> 6
+    spread_w = jnp.where(spread_row == spread_col + 24, 1.0, 0.0).astype(BF16)
+    spread_e = jnp.where(spread_row == spread_col + 32, 1.0, 0.0).astype(BF16)
     upper4 = lax.broadcasted_iota(jnp.int32, (8, HALF), 0) < 4
 
     state[...] = jnp.zeros_like(state)
@@ -526,7 +537,7 @@
     def phase2(j):
         blocks = (2 * j, 2 * j + 1)
         bases = [pl.multiple_of(i * GROUP, GROUP) for i in blocks]
-        weights = [dot(colq[i].astype(BF16), spread_w) for i in blocks]
+        weights = [dot(colq[i], spread_w) for i in blocks]
         b_ts = [b_t.astype(BF16) for b_t in assemble(0, j)]
         weighted = []
         for base, weight in zip(bases, weights):
@@ -576,7 +587,7 @@
         half = zbuf[pl.ds(base, GROUP), :].astype(F32) * 0.5
         gate = half + half * jnp.tanh(half)
         zbuf[pl.ds(base, GROUP), :] = gate.astype(BF16)
-        grown = dot(colq[i].astype(BF16), spread_e)
+        grown = dot(colq[i], spread_e)
         egate[pl.ds(base, GROUP), :] = (gate * grown).astype(BF16)
 
     z_copy.wait()
@@ -835,8 +846,8 @@
             pltpu.VMEM((BLOCKS, STATE, GROUP), BF16),
             pltpu.VMEM((LENGTH, WIDTH), F32),
             pltpu.VMEM((BLOCKS, STATE, WIDTH), F32),
-            pltpu.VMEM((BLOCKS, GROUP, 24), F32),
-            pltpu.VMEM((BLOCKS, 24, GROUP), F32),
+            pltpu.VMEM((BLOCKS, GROUP, 40), BF16),
+            pltpu.VMEM((BLOCKS, 40, GROUP), F32),
             pltpu.VMEM((BLOCKS, 8, GROUP), F32),
             pltpu.VMEM((BLOCKS, 8, GROUP), F32),
             pltpu.VMEM((8, HALF + LENGTH), F32),

time: 66 us -> 65.7 us (level)
  no operation moved by 1% of the time
where the time goes in v6:
time: 65.7 us; the launch traced here: 65.6 us
  Pallas kernels  65.6 us (100%)
    pallas_call x1, Pallas kernels, body(): pl.pallas_call(layer, out_shape=(jax.ShapeDtypeStruct((LENGTH, WIDTH), BF...  61.4 us
    pallas_call x1, Pallas kernels, body(): pl.pallas_call(scale, out_shape=jax.ShapeDtypeStruct((LENGTH, WIDTH), BF1...  4.21 us

profile of v6, /device:TPU:32, one launch (start us, length us, event | category | flops | bytes accessed | tf_op | source)
XLA Modules:
  0.0 65.6 jit_solution(18441205755410221614)
XLA Ops:
  0.0 61.4 %layer.1 = (bf16[5120,384]{1,0:T(8,128)(2,1)}, f32[24,256]{1,0:T(8,128)}) custom-call(bf16[5120,384]{1,0:T(8,128)(2,1)} %x_hbm.1, bf16[5120,384]{1,0:T(8,128)(2,1)} %z_hbm.1, bf16[4,5120]{1,0:T(4,128)(2,1)} %bitcast.4, bf16[4,5120]{1,0:T(4,128)(2,1)} %bitcast.5, f32[6,5120]{1,0:T(8,128)} %bitcast.3, bf16[4,384]{1,0:T(4,128)(2,1)} %taps_ref.1, ...), custom_call_target="tpu_custom_call" | custom-call | tf_op jit(solution)/shard_map/layer/pallas_call | solution.py:828
  61.4 4.2 %scale.1 = bf16[5120,384]{1,0:T(8,128)(2,1)} custom-call(bf16[5120,384]{1,0:T(8,128)(2,1)} %get-tuple-element.7.g_hbm, f32[24,256]{1,0:T(8,128)} %get-tuple-element.8.total_hbm, f32[384]{0:T(512)} %gain_hbm.1), custom_call_target="tpu_custom_call" | custom-call | tf_op jit(solution)/shard_map/scale/pallas_call | solution.py:900

commit v7 on v6

--- a/solution.py
+++ b/solution.py
@@ -486,11 +486,11 @@
         step1,
         {
             5: [(event_side, 0), (event_side, 1), (event_halo,), (send_z, 1, 0)],
-            9: [(event_z, 0, 0)],
-            12: [(event_ring, 0, 1), (event_z, 0, 1), (send_z, 1, 1)],
-            14: [(event_ring, 1, 1), (event_first,)],
-            15: [(event_f, 0, 0)],
-            18: [(event_f, 0, 1), (event_ring, 0, 2)],
+            10: [(event_z, 0, 0)],
+            13: [(event_ring, 0, 1), (event_z, 0, 1), (send_z, 1, 1)],
+            15: [(event_ring, 1, 1), (event_first,)],
+            17: [(event_f, 0, 0)],
+            19: [(event_f, 0, 1), (event_ring, 0, 2)],
         },
     )
 

time: 65.7 us -> 65.2 us (level)
  Pallas kernels: 65.6 us -> 64.7 us
    pallas_call x1, Pallas kernels: 61.4 us -> 60.5 us  [body(): pl.pallas_call(layer, out_shape=(jax.ShapeDtypeStruct((LENGTH, WIDTH), BF...]
where the time goes in v7:
time: 65.2 us; the launch traced here: 64.8 us
  Pallas kernels  64.7 us (99%)
    pallas_call x1, Pallas kernels, body(): pl.pallas_call(layer, out_shape=(jax.ShapeDtypeStruct((LENGTH, WIDTH), BF...  60.5 us
    pallas_call x1, Pallas kernels, body(): pl.pallas_call(scale, out_shape=jax.ShapeDtypeStruct((LENGTH, WIDTH), BF1...  4.21 us

profile of v7, /device:TPU:32, one launch (start us, length us, event | category | flops | bytes accessed | tf_op | source)
XLA Modules:
  0.0 64.8 jit_solution(11386856255755585984)
XLA Ops:
  0.0 60.5 %layer.1 = (bf16[5120,384]{1,0:T(8,128)(2,1)}, f32[24,256]{1,0:T(8,128)}) custom-call(bf16[5120,384]{1,0:T(8,128)(2,1)} %x_hbm.1, bf16[5120,384]{1,0:T(8,128)(2,1)} %z_hbm.1, bf16[4,5120]{1,0:T(4,128)(2,1)} %bitcast.4, bf16[4,5120]{1,0:T(4,128)(2,1)} %bitcast.5, f32[6,5120]{1,0:T(8,128)} %bitcast.3, bf16[4,384]{1,0:T(4,128)(2,1)} %taps_ref.1, ...), custom_call_target="tpu_custom_call" | custom-call | tf_op jit(solution)/shard_map/layer/pallas_call | solution.py:828
  60.5 4.2 %scale.1 = bf16[5120,384]{1,0:T(8,128)(2,1)} custom-call(bf16[5120,384]{1,0:T(8,128)(2,1)} %get-tuple-element.7.g_hbm, f32[24,256]{1,0:T(8,128)} %get-tuple-element.8.total_hbm, f32[384]{0:T(512)} %gain_hbm.1), custom_call_target="tpu_custom_call" | custom-call | tf_op jit(solution)/shard_map/scale/pallas_call | solution.py:900
